TPU v7x, 256 devices: a whole 4x4x8 slice. The times are simulated.
256 devices in a mesh: tensor: 2 (over z_hi), fsdp: 32 (over x, z_lo, core), island: 4 (over y).
Axes of the slice: x: 4, y: 4, z: 8 (z_hi: 2, z_lo: 4; z = z_hi * 4 + z_lo), core: 2. Of those that a mesh axis runs over, the one named last changes fastest.
Arguments:
- activations: bfloat16 [4, 16384, 1024], P('island', 'fsdp', 'tensor'), may hold values from -6 to 6
- out_grads: bfloat16 [4, 16384, 2048], P('island', 'fsdp', 'tensor'), may hold values from -6 to 6
- moment: float32 [4, 2, 1024, 1024], P('island', 'tensor', 'fsdp'), may hold values from -6 to 6
- moment_sq: float32 [4, 2, 1024, 1024], P('island', 'tensor', 'fsdp'), may hold values from 0.05 to 2
- left_factor: float32 [4, 2, 1024, 1024], P('island', 'tensor', 'fsdp'), may hold values from -1 to 7, as said below
- right_factor: float32 [4, 2, 1024, 1024], P('island', 'tensor', 'fsdp'), may hold values from -1 to 7, as said below
- left_basis: bfloat16 [4, 2, 1024, 1024], P('island', 'tensor'), may hold values from -1 to 2
- right_basis: bfloat16 [4, 2, 1024, 1024], P('island', 'tensor'), may hold values from -1 to 2
- params: float32 [4, 2, 1024, 1024], P('island', 'tensor', 'fsdp'), may hold values from -6 to 6
- anchor: float32 [2, 1024, 1024], P('tensor', 'fsdp'), may hold values from -6 to 6
- outer_momentum: float32 [2, 1024, 1024], P('tensor', 'fsdp'), may hold values from -3 to 3
Outputs:
- anchor_new: float32 [2, 1024, 1024], P('tensor', 'fsdp')
- momentum_new: float32 [2, 1024, 1024], P('tensor', 'fsdp')
- moment_new: float32 [4, 2, 1024, 1024], P('island', 'tensor', 'fsdp')
- moment_sq_new: float32 [4, 2, 1024, 1024], P('island', 'tensor', 'fsdp')
- left_factor_new: float32 [4, 2, 1024, 1024], P('island', 'tensor', 'fsdp')
- right_factor_new: float32 [4, 2, 1024, 1024], P('island', 'tensor', 'fsdp')
- left_basis_new: bfloat16 [4, 2, 1024, 1024], P('island', 'tensor')
- right_basis_new: bfloat16 [4, 2, 1024, 1024], P('island', 'tensor')
Inputs may be any that keep to these rules, and one draw needn't show every extreme that they name: `left_factor`: each matrix is symmetric, and each diagonal entry exceeds the sum of magnitudes of the other entries of its row. `right_factor`: each matrix is symmetric, and each diagonal entry exceeds the sum of magnitudes of the other entries of its row.
All inputs are finite; a program needn't handle non-finite values.
Results may differ from a plain program's by a relative error of at most 0.0059.
Values may be sent and summed in bfloat16 or wider, within the bound.
A program may use at most 128 MiB of HBM per device.

v0:
```python
import math

import jax
import jax.numpy as jnp
from jax import lax
from jax.sharding import PartitionSpec as P

BETA_ONE = 0.9
BETA_TWO = 0.95
FACTOR_BETA = 0.9
ADAM_EPS = 1e-08
INNER_RATE = 0.5
OUTER_RATE = 0.7
OUTER_MOMENT = 0.9


def mixed_dot(left, right):
    return jnp.dot(left, right, preferred_element_type=jnp.float32)


def exact_dot(left, right):
    return jnp.dot(left, right, precision=lax.Precision.HIGHEST, preferred_element_type=jnp.float32)


def gram_of(power_all):
    return mixed_dot(power_all.T, power_all)


def blocked_cholesky(grams):
    order = grams.shape[-1]
    half = order // 2
    upper_left = grams[:, :half, :half]
    lower_left = grams[:, half:, :half]
    lower_right = grams[:, half:, half:]
    head = jnp.linalg.cholesky(upper_left)
    panel_t = jax.scipy.linalg.solve_triangular(head, jnp.swapaxes(lower_left, 1, 2), lower=True)
    panel = jnp.swapaxes(panel_t, 1, 2)
    schur = lower_right - jnp.einsum("bik,bjk->bij", panel, panel, precision=lax.Precision.HIGHEST)
    tail = jnp.linalg.cholesky(schur)
    zeros_block = jnp.zeros_like(lower_left)
    top = jnp.concatenate([head, jnp.swapaxes(zeros_block, 1, 2)], axis=2)
    bottom = jnp.concatenate([panel, tail], axis=2)
    return jnp.concatenate([top, bottom], axis=1)


def solve_rows(lower, power_rows):
    solved = jax.scipy.linalg.solve_triangular(lower, power_rows.T.astype(jnp.float32), lower=True)
    return solved.T.astype(jnp.bfloat16)


def per_device(
    activations,
    out_grads,
    moment,
    moment_sq,
    left_factor,
    right_factor,
    left_basis,
    right_basis,
    params,
    anchor,
    outer_momentum,
):
    features = lax.all_gather(activations[0], "tensor", axis=1, tiled=True)
    grad_rows = out_grads[0]
    owners = lax.axis_size("fsdp")
    row_count = left_factor.shape[2]
    block_width = features.shape[1]
    grad_scale = 1.0 / math.sqrt(features.shape[0] * owners)
    first_row = lax.axis_index("fsdp") * row_count
    own_rows = lax.psum_scatter(
        mixed_dot(features.T, grad_rows) * grad_scale, "fsdp", scatter_dimension=0, tiled=True
    ).astype(jnp.bfloat16)
    gradient_full = lax.all_gather(own_rows, "fsdp", axis=0, tiled=True)
    left_old = left_basis[0, 0]
    right_old = right_basis[0, 0]
    left_columns = lax.dynamic_slice_in_dim(left_old, first_row, row_count, 1)
    half_turn = mixed_dot(left_columns.T, gradient_full).astype(jnp.bfloat16)
    rotated = mixed_dot(half_turn, right_old)
    first_moment = BETA_ONE * moment[0, 0] + (1.0 - BETA_ONE) * rotated
    second_moment = BETA_TWO * moment_sq[0, 0] + (1.0 - BETA_TWO) * rotated * rotated
    normed = (first_moment / (jnp.sqrt(second_moment) + ADAM_EPS)).astype(jnp.bfloat16)
    own_columns = lax.dynamic_slice_in_dim(gradient_full, first_row, row_count, 1)
    left_next = (
        FACTOR_BETA * left_factor[0, 0]
        + (1.0 - FACTOR_BETA) * mixed_dot(own_rows, gradient_full.T) / block_width
    )
    right_next = (
        FACTOR_BETA * right_factor[0, 0]
        + (1.0 - FACTOR_BETA) * mixed_dot(own_columns.T, gradient_full) / block_width
    )
    power_left = mixed_dot(left_next.astype(jnp.bfloat16), left_old).astype(jnp.bfloat16)
    power_right = mixed_dot(right_next.astype(jnp.bfloat16), right_old).astype(jnp.bfloat16)
    normed_all, power_left_all, power_right_all = (
        lax.all_gather(normed, "fsdp", axis=0, tiled=True),
        lax.all_gather(power_left, "fsdp", axis=0, tiled=True),
        lax.all_gather(power_right, "fsdp", axis=0, tiled=True),
    )
    left_rows = lax.dynamic_slice_in_dim(left_old, first_row, row_count, 0)
    back_half = mixed_dot(left_rows, normed_all).astype(jnp.bfloat16)
    update = mixed_dot(back_half, right_old.T)
    lowers = blocked_cholesky(jnp.stack([gram_of(power_left_all), gram_of(power_right_all)]))
    lower_left = lowers[0]
    lower_right = lowers[1]
    fresh_left = solve_rows(lower_left, power_left)
    fresh_right = solve_rows(lower_right, power_right)
    left_new, right_new = (
        lax.all_gather(fresh_left, "fsdp", axis=0, tiled=True),
        lax.all_gather(fresh_right, "fsdp", axis=0, tiled=True),
    )
    turn_right = mixed_dot(right_old.T, right_new)
    carried_rows = exact_dot(first_moment, turn_right)
    carried_all = lax.all_gather(carried_rows, "fsdp", axis=0, tiled=True)
    new_columns = lax.dynamic_slice_in_dim(left_new, first_row, row_count, 1)
    turn_rows = mixed_dot(new_columns.T, left_old)
    moment_next = exact_dot(turn_rows, carried_all)
    island_delta = anchor[0] - (params[0, 0] - INNER_RATE * update)
    average = lax.psum(island_delta, "island") / lax.axis_size("island")
    momentum_next = OUTER_MOMENT * outer_momentum[0] + average
    anchor_next = anchor[0] - OUTER_RATE * (average + OUTER_MOMENT * momentum_next)
    return (
        anchor_next[None],
        momentum_next[None],
        moment_next[None, None],
        second_moment[None, None],
        left_next[None, None],
        right_next[None, None],
        left_new[None, None],
        right_new[None, None],
    )


def solution(mesh):
    in_specs = (
        P("island", "fsdp", "tensor"),
        P("island", "fsdp", "tensor"),
        P("island", "tensor", "fsdp", None),
        P("island", "tensor", "fsdp", None),
        P("island", "tensor", "fsdp", None),
        P("island", "tensor", "fsdp", None),
        P("island", "tensor", None, None),
        P("island", "tensor", None, None),
        P("island", "tensor", "fsdp", None),
        P("tensor", "fsdp", None),
        P("tensor", "fsdp", None),
    )
    out_specs = (
        P("tensor", "fsdp", None),
        P("tensor", "fsdp", None),
        P("island", "tensor", "fsdp", None),
        P("island", "tensor", "fsdp", None),
        P("island", "tensor", "fsdp", None),
        P("island", "tensor", "fsdp", None),
        P("island", "tensor", None, None),
        P("island", "tensor", None, None),
    )
    return jax.shard_map(
        per_device, mesh=mesh, in_specs=in_specs, out_specs=out_specs, check_vma=False
    )
```

profile of v0, /device:TPU:32, one launch (start us, length us, event | category | flops | bytes accessed | tf_op | source)
XLA Modules:
  0.0 1305.8 jit_solution(17011572401583944737)
XLA Ops:
  8.0 45.3 %all-gather.24.cloned.1.call-done = bf16[1,512,1024]{2,1,0:T(8,128)(2,1)} async-done(((bf16[1,512,512]{2,1,0:T(8,128)(2,1)}), bf16[1,512,1024]{2,1,0:T(8,128)(2,1)}) %all-gather.24.cloned.1.call-update) | async-done | bytes 1048592 | tf_op jit(solution)/shard_map/all_gather | solution.py:64
  53.2 4.8 convolution_multiply_fusion
  58.1 144.5 %reduce-scatter.2.cloned.1.call-done = f32[32,1024]{1,0:T(8,128)} async-done(((f32[1024,1024]{1,0:T(8,128)}), f32[32,1024]{1,0:T(8,128)}) %reduce-scatter.2.cloned.1.call-update) | async-done | bytes 131088 | tf_op jit(solution)/shard_map/reduce_scatter | solution.py:71
  204.3 62.8 %all-gather.10.cloned.1.call-done = bf16[1024,1024]{1,0:T(8,128)(2,1)} async-done(((bf16[32,1024]{1,0:T(8,128)(2,1)}), bf16[1024,1024]{1,0:T(8,128)(2,1)}) %all-gather.10.cloned.1.call-update) | async-done | bytes 2097168 | tf_op jit(solution)/shard_map/all_gather | solution.py:74
  278.0 2.7 fusion.15
  281.6 48.9 %all-gather.16.cloned.1.call-done = bf16[1024,1024]{1,0:T(8,128)(2,1)} async-done(((bf16[32,1024]{1,0:T(8,128)(2,1)}), bf16[1024,1024]{1,0:T(8,128)(2,1)}) %all-gather.16.cloned.1.call-update) | async-done | bytes 2097168 | tf_op jit(solution)/shard_map/all_gather | solution.py:97
  330.5 6.6 convolution_bitcast_fusion
  337.1 54.8 %all-gather.14.cloned.1.call-done = bf16[1024,1024]{1,0:T(8,128)(2,1)} async-done(((bf16[32,1024]{1,0:T(8,128)(2,1)}), bf16[1024,1024]{1,0:T(8,128)(2,1)}) %all-gather.14.cloned.1.call-update) | async-done | bytes 2097168 | tf_op jit(solution)/shard_map/all_gather | solution.py:96
  391.8 4.8 convolution_bitcast_fusion.1
  396.6 3.0 maximum_bitcast_fusion
  399.9 3.2 copy.53
  403.1 2.8 fusion.4
  407.3 23.5 %custom-call.40 = f32[2,128,128]{2,1,0:T(8,128)S(1)} custom-call(f32[2,128,128]{2,1,0:T(8,128)S(1)} %cholesky.430), custom_call_target="Cholesky" | custom-call | tf_op jit(solution)/shard_map/jit(cholesky)/cholesky | solution.py:35
  432.3 19.7 %custom-call.41 = f32[2,1,128,128]{2,3,1,0:T(8,128)S(1)} custom-call(f32[2,1,128,128]{3,2,1,0:T(8,128)S(1)} %select_bitcast_fusion.5), custom_call_target="InvertDiagBlocksLowerTriangular" | custom-call | tf_op jit(solution)/shard_map/jit(cholesky)/cholesky | solution.py:35
  455.8 23.5 %custom-call.42 = f32[2,128,128]{2,1,0:T(8,128)S(1)} custom-call(f32[2,128,128]{2,1,0:T(8,128)S(1)} %cholesky.434), custom_call_target="Cholesky" | custom-call | tf_op jit(solution)/shard_map/jit(cholesky)/cholesky | solution.py:35
  479.9 20.1 %custom-call.43 = f32[2,1,128,128]{2,3,1,0:T(8,128)S(1)} custom-call(f32[2,1,128,128]{3,2,1,0:T(8,128)S(1)} %get-tuple-element.90), custom_call_target="InvertDiagBlocksLowerTriangular" | custom-call | tf_op jit(solution)/shard_map/jit(cholesky)/cholesky | solution.py:35
  502.9 23.5 %custom-call.44 = f32[2,128,128]{2,1,0:T(8,128)S(1)} custom-call(f32[2,128,128]{2,1,0:T(8,128)S(1)} %cholesky.439), custom_call_target="Cholesky" | custom-call | tf_op jit(solution)/shard_map/jit(cholesky)/cholesky | solution.py:35
  527.0 19.7 %custom-call.45 = f32[2,1,128,128]{2,3,1,0:T(8,128)S(1)} custom-call(f32[2,1,128,128]{3,2,1,0:T(8,128)S(1)} %get-tuple-element.88), custom_call_target="InvertDiagBlocksLowerTriangular" | custom-call | tf_op jit(solution)/shard_map/jit(cholesky)/cholesky | solution.py:35
  549.4 23.6 %custom-call.46 = f32[2,128,128]{2,1,0:T(8,128)S(1)} custom-call(f32[2,128,128]{2,1,0:T(8,128)S(1)} %convolution_subtract_fusion.7), custom_call_target="Cholesky" | custom-call | tf_op jit(solution)/shard_map/jit(cholesky)/cholesky | solution.py:35
  574.1 4.3 broadcast_select_fusion
  578.4 14.4 %while.5 = (s32[]{:T(128)}, f32[2,512,512]{2,1,0:T(8,128)}, s32[4,2]{0,1:T(2,128)S(1)}, f32[4,2,128,128]{3,2,0,1:T(8,128)}, s32[]{:T(128)}) while((s32[]{:T(128)}, f32[2,512,512]{2,1,0:T(8,128)}, s32[4,2]{0,1:T(2,128)S(1)}, f32[4,2,128,128]{3,2,0,1:T(8,128)}, s32[]{:T(128)}) %tuple.118), condition=%wide.while_cond.1, body=%wide.while_body.1.sunk | while | flops 2 | bytes 263277 | solution.py:36
  578.9 3.0 bitcast_dynamic-update-slice_fusion.6
  582.6 3.0 bitcast_dynamic-update-slice_fusion.6
  586.2 3.0 bitcast_dynamic-update-slice_fusion.6
  589.8 3.0 bitcast_dynamic-update-slice_fusion.6
  592.7 79.6 %custom-call.31 = f32[2,4,128,128]{2,3,1,0:T(8,128)S(1)} custom-call(f32[2,4,128,128]{3,2,1,0:T(8,128)} %bitcast.324), custom_call_target="InvertDiagBlocksLowerTriangular" | custom-call | tf_op jit(solution)/shard_map/jit(_solve_triangular)/vmap()/triangular_solve | solution.py:36
  681.6 2.9 fusion.23
  691.5 7.0 fusion.2
  698.5 2.9 copy.71
  705.4 23.9 %custom-call.47 = f32[2,128,128]{2,1,0:T(8,128)S(1)} custom-call(f32[2,128,128]{2,1,0:T(8,128)S(1)} %cholesky.443), custom_call_target="Cholesky" | custom-call | tf_op jit(solution)/shard_map/jit(cholesky)/cholesky | solution.py:39
  730.0 20.3 %custom-call.48 = f32[2,1,128,128]{2,3,1,0:T(8,128)} custom-call(f32[2,1,128,128]{3,2,1,0:T(8,128)S(1)} %select_bitcast_fusion.2), custom_call_target="InvertDiagBlocksLowerTriangular" | custom-call | tf_op jit(solution)/shard_map/jit(cholesky)/cholesky | solution.py:39
  758.1 23.5 %custom-call.49 = f32[2,128,128]{2,1,0:T(8,128)S(1)} custom-call(f32[2,128,128]{2,1,0:T(8,128)S(1)} %slice-done), custom_call_target="Cholesky" | custom-call | tf_op jit(solution)/shard_map/jit(cholesky)/cholesky | solution.py:39
  784.6 19.8 %custom-call.50 = f32[2,1,128,128]{2,3,1,0:T(8,128)S(1)} custom-call(f32[2,1,128,128]{3,2,1,0:T(8,128)S(1)} %get-tuple-element.85), custom_call_target="InvertDiagBlocksLowerTriangular" | custom-call | tf_op jit(solution)/shard_map/jit(cholesky)/cholesky | solution.py:39
  807.4 23.5 %custom-call.51 = f32[2,128,128]{2,1,0:T(8,128)S(1)} custom-call(f32[2,128,128]{2,1,0:T(8,128)S(1)} %cholesky.452), custom_call_target="Cholesky" | custom-call | tf_op jit(solution)/shard_map/jit(cholesky)/cholesky | solution.py:39
  831.5 19.7 %custom-call.52 = f32[2,1,128,128]{2,3,1,0:T(8,128)S(1)} custom-call(f32[2,1,128,128]{3,2,1,0:T(8,128)S(1)} %get-tuple-element.83), custom_call_target="InvertDiagBlocksLowerTriangular" | custom-call | tf_op jit(solution)/shard_map/jit(cholesky)/cholesky | solution.py:39
  853.9 23.7 %custom-call.53 = f32[2,128,128]{2,1,0:T(8,128)S(1)} custom-call(f32[2,128,128]{2,1,0:T(8,128)S(1)} %convolution_subtract_fusion.6), custom_call_target="Cholesky" | custom-call | tf_op jit(solution)/shard_map/jit(cholesky)/cholesky | solution.py:39
  882.7 4.2 fusion
  887.0 23.2 %while.7 = (s32[]{:T(128)}, f32[1024,1024]{1,0:T(8,128)}, s32[8,2]{0,1:T(2,128)S(1)}, f32[8,128,128]{2,1,0:T(8,128)S(1)}, s32[]{:T(128)}) while((s32[]{:T(128)}, f32[1024,1024]{1,0:T(8,128)}, s32[8,2]{0,1:T(2,128)S(1)}, f32[8,128,128]{2,1,0:T(8,128)S(1)}, s32[]{:T(128)}) %tuple.124), condition=%wide.while_cond.clone, body=%wide.while_body.clone.sunk | while | flops 2 | bytes 131189 | solution.py:47
  910.2 78.6 %custom-call.55 = f32[8,128,128]{1,2,0:T(8,128)S(1)} custom-call(f32[8,128,128]{2,1,0:T(8,128)S(1)} %get-tuple-element.33), custom_call_target="InvertDiagBlocksLowerTriangular" | custom-call | tf_op jit(solution)/shard_map/jit(_solve_triangular)/triangular_solve | solution.py:47
  1000.3 23.5 %while.6 = (s32[]{:T(128)}, f32[1024,1024]{1,0:T(8,128)}, s32[8,2]{0,1:T(2,128)S(1)}, f32[8,128,128]{2,1,0:T(8,128)S(1)}, s32[]{:T(128)}) while((s32[]{:T(128)}, f32[1024,1024]{1,0:T(8,128)}, s32[8,2]{0,1:T(2,128)S(1)}, f32[8,128,128]{2,1,0:T(8,128)S(1)}, s32[]{:T(128)}) %tuple.149), condition=%wide.while_cond, body=%wide.while_body.sunk | while | flops 2 | bytes 131189 | solution.py:47
  1023.8 78.6 %custom-call.54 = f32[8,128,128]{1,2,0:T(8,128)S(1)} custom-call(f32[8,128,128]{2,1,0:T(8,128)S(1)} %get-tuple-element.32), custom_call_target="InvertDiagBlocksLowerTriangular" | custom-call | tf_op jit(solution)/shard_map/jit(_solve_triangular)/triangular_solve | solution.py:47
  1113.0 3.4 fusion.34
  1117.7 4.0 fusion.9
  1121.8 4.6 fusion.146
  1126.4 35.8 %all-reduce.4.cloned.1.call-done = f32[32,1024]{1,0:T(8,128)} async-done(((f32[32,1024]{1,0:T(8,128)}), f32[32,1024]{1,0:T(8,128)}) %all-reduce.4.cloned.1.call-update) | async-done | bytes 131088 | tf_op jit(solution)/shard_map/psum | solution.py:118
  1163.8 61.2 %all-gather.18.cloned.1.call-done = bf16[1024,1024]{1,0:T(8,128)(2,1)} async-done(((bf16[32,1024]{1,0:T(8,128)(2,1)}), bf16[1024,1024]{1,0:T(8,128)(2,1)}) %all-gather.18.cloned.1.call-update) | async-done | bytes 2097168 | tf_op jit(solution)/shard_map/all_gather | solution.py:108
  1227.3 62.0 %all-gather.22.cloned.1.call-done = f32[1024,1024]{1,0:T(8,128)} async-done(((f32[32,1024]{1,0:T(8,128)}), f32[1024,1024]{1,0:T(8,128)}) %all-gather.22.cloned.1.call-update) | async-done | bytes 4194320 | tf_op jit(solution)/shard_map/all_gather | solution.py:113
  1289.3 5.5 convolution_bitcast_fusion.2
  (268 shorter events, 151.3 us)
Async XLA Ops:
  7.2 263.0 %copy-start = (bf16[1,1,1024,1024]{3,2,1,0:T(8,128)(2,1)S(1)}, bf16[1,1,1024,1024]{3,2,1,0:T(8,128)(2,1)}, u32[]{:S(2)}) copy-start(bf16[1,1,1024,1024]{3,2,1,0:T(8,128)(2,1)} %param.21) | copy-start | bytes 6291460
  7.2 46.0 %all-gather.24.cloned.1.call-start = ((), (), s32[]{:S(2)}) async-start(), calls=%async_computation.10 | async-start | bytes 1572864 | tf_op jit(solution)/shard_map/all_gather | solution.py:64
  7.9 194.8 %reduce-scatter.2.cloned.1.call-start = ((), (), s32[]{:S(2)}) async-start(), calls=%async_computation.1 | async-start | bytes 4325376 | tf_op jit(solution)/shard_map/reduce_scatter | solution.py:71
  58.0 209.1 %copy-start.35 = (f32[1,1,32,1024]{3,2,1,0:T(8,128)S(1)}, f32[1,1,32,1024]{3,2,1,0:T(8,128)}, u32[]{:S(2)}) copy-start(f32[1,1,32,1024]{3,2,1,0:T(8,128)} %param.19) | copy-start | bytes 393220
  58.1 209.1 %all-gather.10.cloned.1.call-start = ((), (), s32[]{:S(2)}) async-start(), calls=%async_computation.2 | async-start | bytes 2162688 | tf_op jit(solution)/shard_map/all_gather | solution.py:74
  204.2 126.2 %all-gather.16.cloned.1.call-start = ((), (), s32[]{:S(2)}) async-start(), calls=%async_computation.6 | async-start | bytes 2162688 | tf_op jit(solution)/shard_map/all_gather | solution.py:97
  204.3 67.0 %copy-start.23 = (bf16[32,1024]{1,0:T(8,128)(2,1)S(1)}, bf16[32,1024]{1,0:T(8,128)(2,1)}, u32[]{:S(2)}) copy-start(bf16[32,1024]{1,0:T(8,128)(2,1)} %convert_element_type.52) | copy-start | bytes 196612
  204.3 67.0 %copy-start.36 = (f32[1,1,32,1024]{3,2,1,0:T(8,128)S(1)}, f32[1,1,32,1024]{3,2,1,0:T(8,128)}, u32[]{:S(2)}) copy-start(f32[1,1,32,1024]{3,2,1,0:T(8,128)} %param.18) | copy-start | bytes 393220
  271.2 6.1 copy-start.24
  271.3 120.6 %all-gather.14.cloned.1.call-start = ((), (), s32[]{:S(2)}) async-start(), calls=%async_computation.5 | async-start | bytes 2162688 | tf_op jit(solution)/shard_map/all_gather | solution.py:96
  271.3 2.5 copy-start.3
  273.8 1.8 copy-start.28
  275.0 838.0 %all-gather.12.cloned.1.call-start = ((), (), s32[]{:S(2)}) async-start(), calls=%async_computation.3 | async-start | bytes 2162688 | tf_op jit(solution)/shard_map/all_gather | solution.py:95
  275.6 297.4 %copy-start.33 = (pred[128,128]{1,0:T(8,128)(4,1)}, pred[128,128]{1,0:T(8,128)(4,1)S(1)}, u32[]{:S(2)}) copy-start(pred[128,128]{1,0:T(8,128)(4,1)S(1)} %iota_compare_fusion.4) | copy-start | bytes 49156
  275.7 298.3 %copy-start.14 = (pred[512,512]{1,0:T(8,128)(4,1)}, pred[512,512]{1,0:T(8,128)(4,1)S(1)}, u32[]{:S(2)}) copy-start(pred[512,512]{1,0:T(8,128)(4,1)S(1)} %iota_compare_fusion.2) | copy-start | bytes 786436
  278.0 2.8 copy-start.31
  278.0 2.8 copy-start.39
  280.8 56.3 %copy-start.19 = (f32[32,1024]{1,0:T(8,128)}, f32[32,1024]{1,0:T(8,128)S(1)}, u32[]{:S(2)}) copy-start(f32[32,1024]{1,0:T(8,128)S(1)} %fusion.15) | copy-start | bytes 393220
  281.5 836.2 %all-gather.20.cloned.1.call-start = ((), (), s32[]{:S(2)}) async-start(), calls=%async_computation.8 | async-start | bytes 2162688 | tf_op jit(solution)/shard_map/all_gather | solution.py:109
  391.8 4.8 copy-start.1
  396.6 3.3 copy-start.2
  405.8 1.4 copy-start.8
  672.4 1.9 copy-start.25
  672.4 5.2 copy-start.6
  687.5 3.9 copy-start.10
  704.1 1.3 copy-start.7
  705.4 50.0 %copy-start.11 = (f32[2,128,512]{1,2,0:T(8,128)S(1)}, f32[2,128,512]{1,2,0:T(8,128)}, u32[]{:S(2)}) copy-start(f32[2,128,512]{1,2,0:T(8,128)} %copy.66) | copy-start | bytes 1572868
  755.4 2.7 slice-start
  755.4 26.2 %copy-start.22 = (f32[2,128,128]{2,1,0:T(8,128)S(1)}, f32[2,128,128]{2,1,0:T(8,128)}, u32[]{:S(2)}) copy-start(f32[2,128,128]{2,1,0:T(8,128)} %copy-done.21) | copy-start | bytes 393220
  758.1 25.1 %copy-start.17 = (f32[2,384,128]{2,1,0:T(8,128)S(1)}, f32[2,384,128]{2,1,0:T(8,128)}, u32[]{:S(2)}) copy-start(f32[2,384,128]{2,1,0:T(8,128)} %copy.76) | copy-start | bytes 1179652
  758.1 46.3 %copy-start.18 = (f32[2,384,128]{2,1,0:T(8,128)S(1)}, f32[2,384,128]{2,1,0:T(8,128)}, u32[]{:S(2)}) copy-start(f32[2,384,128]{2,1,0:T(8,128)} %convolution_subtract_fusion.2) | copy-start | bytes 1179652
  784.0 93.6 %copy-start.34 = (pred[128,128]{1,0:T(8,128)(4,1)S(1)}, pred[128,128]{1,0:T(8,128)(4,1)}, u32[]{:S(2)}) copy-start(pred[128,128]{1,0:T(8,128)(4,1)} %copy-done.33) | copy-start | bytes 49156
  804.5 74.3 %copy-start.15 = (pred[512,512]{1,0:T(8,128)(4,1)S(1)}, pred[512,512]{1,0:T(8,128)(4,1)}, u32[]{:S(2)}) copy-start(pred[512,512]{1,0:T(8,128)(4,1)} %copy-done.14) | copy-start | bytes 786436
  878.8 2.2 copy-start.4
  878.8 2.8 copy-start.5
  882.7 4.2 copy-start.42
  882.7 106.1 %copy-start.30 = (f32[1024,32]{0,1:T(8,128)S(1)}, f32[1024,32]{0,1:T(8,128)}, u32[]{:S(2)}) copy-start(f32[1024,32]{0,1:T(8,128)} %convert_bitcast_fusion) | copy-start | bytes 393220
  992.8 109.6 %copy-start.29 = (f32[1024,32]{0,1:T(8,128)S(1)}, f32[1024,32]{0,1:T(8,128)}, u32[]{:S(2)}) copy-start(f32[1024,32]{0,1:T(8,128)} %convert_bitcast_fusion.1) | copy-start | bytes 393220
  1000.2 161.9 %all-reduce.4.cloned.1.call-start = ((), (), s32[]{:S(2)}) async-start(), calls=%async_computation.4 | async-start | bytes 262144 | tf_op jit(solution)/shard_map/psum | solution.py:118
  1000.3 112.7 %copy-start.26 = (f32[1,32,1024]{2,1,0:T(8,128)S(1)}, f32[1,32,1024]{2,1,0:T(8,128)}, u32[]{:S(2)}) copy-start(f32[1,32,1024]{2,1,0:T(8,128)} %param.23) | copy-start | bytes 393220
  1000.3 112.7 %copy-start.37 = (f32[1,1,32,1024]{3,2,1,0:T(8,128)S(1)}, f32[1,1,32,1024]{3,2,1,0:T(8,128)}, u32[]{:S(2)}) copy-start(f32[1,1,32,1024]{3,2,1,0:T(8,128)} %param.22) | copy-start | bytes 393220
  1116.5 108.6 %all-gather.18.cloned.1.call-start = ((), (), s32[]{:S(2)}) async-start(), calls=%async_computation.7 | async-start | bytes 2162688 | tf_op jit(solution)/shard_map/all_gather | solution.py:108
  1117.3 4.4 copy-start.20
  1117.4 4.4 copy-start.32
  1117.4 171.9 %all-gather.22.cloned.1.call-start = ((), (), s32[]{:S(2)}) async-start(), calls=%async_computation.9 | async-start | bytes 4325376 | tf_op jit(solution)/shard_map/all_gather | solution.py:113
  1121.8 40.4 %copy-start.38 = (f32[1,32,1024]{2,1,0:T(8,128)S(1)}, f32[1,32,1024]{2,1,0:T(8,128)}, u32[]{:S(2)}) copy-start(f32[1,32,1024]{2,1,0:T(8,128)} %param.24) | copy-start | bytes 393220
  1289.3 5.5 copy-start.13
  1294.8 2.3 copy-start.16
  (6 other events, 4.2 us)
Sparse Core Ops, SparseCore 0:
  9.8 43.3 all-gather.23
  58.2 144.4 reduce-scatter.1
  205.1 61.9 all-gather.9
  271.4 59.0 all-gather.15
  332.7 59.0 all-gather.13
  393.5 59.4 all-gather.11
  1000.3 59.8 all-gather.19
  1116.6 45.5 all-reduce.3
  1164.7 60.2 all-gather.17
  1227.4 61.8 all-gather.21
where the time goes:
time: 1320 us; the launch traced here: 1310 us
  other arithmetic  579 us (44%)
  waiting for transfers between devices  516 us (39%)
  matrix products  106 us (8%)
  local copies, waits for them, and re-layouts  87.3 us (7%)
  between operations  15.7 us (1%)
    another operation x4, other arithmetic, solve_rows(): jax.scipy.linalg.solve_triangular(lower, power_rows.T.astype(jnp.float32)...  162 us
    another operation x16, other arithmetic, blocked_cholesky(): tail = jnp.linalg.cholesky(schur)  157 us
    another operation x16, other arithmetic, blocked_cholesky(): head = jnp.linalg.cholesky(upper_left)  156 us
    reduce_scatter x1, waiting for transfers between devices, per_device(): lax.psum_scatter(mixed_dot(features.T, grad_rows) * grad_scale, 'fsdp', s...  145 us
    another operation x3, other arithmetic, blocked_cholesky(): jax.scipy.linalg.solve_triangular(head, jnp.swapaxes(lower_left, 1, 2), l...  83.9 us
    all_gather x1, waiting for transfers between devices, per_device(): gradient_full = lax.all_gather(own_rows, 'fsdp', axis=0, tiled=True)  62.8 us
    all_gather x1, waiting for transfers between devices, per_device(): carried_all = lax.all_gather(carried_rows, 'fsdp', axis=0, tiled=True)  62 us
    all_gather x1, waiting for transfers between devices, per_device(): lax.all_gather(fresh_left, 'fsdp', axis=0, tiled=True)  61.2 us
  transfers between devices with their start and end apart: 10, of which 8 were waited for; matrix products, arithmetic and copies ran while one was open for 57% of the time, Pallas kernels for 0%

commit v1 on v0

--- a/solution.py
+++ b/solution.py
@@ -3,6 +3,8 @@
 import jax
 import jax.numpy as jnp
 from jax import lax
+from jax.experimental import pallas as pl
+from jax.experimental.pallas import tpu as pltpu
 from jax.sharding import PartitionSpec as P
 
 BETA_ONE = 0.9
@@ -12,18 +14,196 @@
 INNER_RATE = 0.5
 OUTER_RATE = 0.7
 OUTER_MOMENT = 0.9
+RESIDUAL_LIMIT = 0.06
+
+N = 1024
+H = 512
+Q4 = 256
+ROUGH = 4
+
+
+def nn(a, b):
+    return jnp.dot(a, b, preferred_element_type=jnp.float32)
+
+
+def nt(a, b):
+    return lax.dot_general(a, b, (((1,), (1,)), ((), ())), preferred_element_type=jnp.float32)
+
+
+def split(x):
+    hi = x.astype(jnp.bfloat16)
+    return hi, (x - hi.astype(jnp.float32)).astype(jnp.bfloat16)
+
+
+def nt3(a, b):
+    return nt(a[0], b[0]) + (nt(a[0], b[1]) + nt(a[1], b[0]))
+
+
+def nn3(a, b):
+    return nn(a[0], b[0]) + (nn(a[0], b[1]) + nn(a[1], b[0]))
+
+
+def iotas(n):
+    return lax.broadcasted_iota(jnp.int32, (n, n), 0), lax.broadcasted_iota(jnp.int32, (n, n), 1)
+
+
+def low(e):
+    r, c = iotas(e.shape[0])
+    return jnp.where(r > c, e, jnp.where(r == c, 0.5 * e, 0.0))
+
+
+def minus_eye(e):
+    r, c = iotas(e.shape[0])
+    return jnp.where(r == c, e - 1.0, e)
+
+
+def diag_rows(s):
+    r, c = iotas(s.shape[0])
+    picked = jnp.where(r == c, s, 0.0)
+    return jnp.sum(picked, 1, keepdims=True), jnp.sum(picked, 0, keepdims=True)
+
+
+def residual(x, s, y_ref):
+    a, b = slice(0, Q4), slice(Q4, H)
+    if len(x) == 1:
+        xa, x2 = x[0][a, a], x[0][b, :]
+        ya = nn(xa, s[0][a, a]).astype(jnp.bfloat16)
+        y2 = nn(x2, s[0][...]).astype(jnp.bfloat16)
+        return nt(ya, xa), nt(y2[:, a], xa), nt(y2, x2)
+    xa = (x[0][a, a], x[1][a, a])
+    x2 = (x[0][b, :], x[1][b, :])
+    ya = split(nn3(xa, (s[0][a, a], s[1][a, a])))
+    y2 = split(nn3(x2, (s[0][...], s[1][...])))
+    y2a = (y2[0][:, a], y2[1][:, a])
+    return nt3(ya, xa), nt3(y2a, xa), nt3(y2, x2)
+
+
+def leaf(s_ref, x_ref, sh, sl, xh, xl):
+    a, b = slice(0, Q4), slice(Q4, H)
+    dc, dr = diag_rows(s_ref[...])
+    dc, dr = lax.rsqrt(dc), lax.rsqrt(dr)
+    sn = s_ref[...] * dc * dr
+    hi, lo = split(sn)
+    sh[...] = hi
+    sl[...] = lo
+    e0 = minus_eye(sn)
+    f0 = low(e0)
+    r, c = iotas(H)
+    x0 = jnp.where(r == c, 1.0 - f0, -f0)
+    x_ref[...] = x0
+    xh[...] = x0.astype(jnp.bfloat16)
+
+    def update(e, fine):
+        eaa, eca, edd = e
+        faa, fdd = low(eaa).astype(jnp.bfloat16), low(edd).astype(jnp.bfloat16)
+        fca = eca.astype(jnp.bfloat16)
+        xa, xc, xd = xh[a, a], xh[b, a], xh[b, b]
+        na = x_ref[a, a] - nn(faa, xa)
+        nc = x_ref[b, a] - (nn(fca, xa) + nn(fdd, xc))
+        nd = x_ref[b, b] - nn(fdd, xd)
+        x_ref[a, a] = na
+        x_ref[b, a] = nc
+        x_ref[b, b] = nd
+        if not fine:
+            xh[a, a] = na.astype(jnp.bfloat16)
+            xh[b, a] = nc.astype(jnp.bfloat16)
+            xh[b, b] = nd.astype(jnp.bfloat16)
+
+    def step(_, carry):
+        eaa, eca, edd = residual((xh,), (sh,), None)
+        update((minus_eye(eaa), eca, minus_eye(edd)), False)
+        return carry
+
+    lax.fori_loop(0, ROUGH, step, 0)
+    hi, lo = split(x_ref[...])
+    xh[...] = hi
+    xl[...] = lo
+    eaa, eca, edd = residual((xh, xl), (sh, sl), None)
+    eaa, edd = minus_eye(eaa), minus_eye(edd)
+    left = jnp.sum(eaa * eaa) + 2.0 * jnp.sum(eca * eca) + jnp.sum(edd * edd)
+    update((eaa, eca, edd), True)
+    x_ref[...] = x_ref[...] * dr
+    hi, lo = split(x_ref[...])
+    xh[...] = hi
+    xl[...] = lo
+    return left
+
+
+def orth_body(p_ref, q_ref, res_ref, pt, s_ref, a21, x_ref, sh, sl, xh, xl, l21h, l21l):
+    f, g = slice(0, H), slice(H, N)
+    a, b = slice(0, Q4), slice(Q4, H)
+    pt[...] = p_ref[...].T
+    s_ref[...] = nt(pt[f, :], pt[f, :])
+    a21[...] = nt(pt[g, :], pt[f, :])
+    r1 = leaf(s_ref, x_ref, sh, sl, xh, xl)
+
+    def by_x(t):
+        ta = tuple(v[:, a] for v in t)
+        xa, x2 = (xh[a, a], xl[a, a]), (xh[b, :], xl[b, :])
+        if len(t) == 1:
+            return nt(ta[0], xa[0]) + nt(ta[0], xa[1]), nt(t[0], x2[0]) + nt(t[0], x2[1])
+        return nt3(ta, xa), nt3(t, x2)
+
+    def l_rows(i, c):
+        rows = pl.ds(pl.multiple_of(i * Q4, Q4), Q4)
+        u, v = by_x(split(a21[rows, :]))
+        uh, ul = split(u)
+        vh, vl = split(v)
+        l21h[rows, a] = uh
+        l21h[rows, b] = vh
+        l21l[rows, a] = ul
+        l21l[rows, b] = vl
+        return c
+    lax.fori_loop(0, 2, l_rows, 0)
+
+    def q1_rows(i, c):
+        rows = pl.ds(pl.multiple_of(i * Q4, Q4), Q4)
+        u, v = by_x((p_ref[rows, f],))
+        uh, ul = split(u)
+        vh, vl = split(v)
+        q_ref[rows, a] = uh
+        q_ref[rows, Q4:H] = vh
+        pt[rows, a] = ul
+        pt[rows, Q4:H] = vl
+        return c
+
+    s_ref[...] = nt(pt[g, :], pt[g, :]) - nt3((l21h[...], l21l[...]), (l21h[...], l21l[...]))
+    lax.fori_loop(0, 4, q1_rows, 0)
+    r2 = leaf(s_ref, x_ref, sh, sl, xh, xl)
+
+    def q2_rows(i, c):
+        rows = pl.ds(pl.multiple_of(i * Q4, Q4), Q4)
+        t = p_ref[rows, g].astype(jnp.float32) - nt3((q_ref[rows, f], pt[rows, f]), (l21h[...], l21l[...]))
+        u, v = by_x(split(t))
+        q_ref[rows, H:H + Q4] = u.astype(jnp.bfloat16)
+        q_ref[rows, H + Q4:N] = v.astype(jnp.bfloat16)
+        return c
+    lax.fori_loop(0, 4, q2_rows, 0)
+    res_ref[...] = jnp.full((8, 128), jnp.maximum(r1, r2), jnp.float32)
+
+
+def orth(p):
+    bf, f32 = jnp.bfloat16, jnp.float32
+    return pl.pallas_call(
+        orth_body,
+        out_shape=(jax.ShapeDtypeStruct((N, N), bf), jax.ShapeDtypeStruct((8, 128), f32)),
+        in_specs=[pl.BlockSpec(memory_space=pltpu.VMEM)],
+        out_specs=(pl.BlockSpec(memory_space=pltpu.VMEM),) * 2,
+        scratch_shapes=[
+            pltpu.VMEM((N, N), bf), pltpu.VMEM((H, H), f32), pltpu.VMEM((H, H), f32), pltpu.VMEM((H, H), f32),
+        ] + [pltpu.VMEM((H, H), bf)] * 6,
+        compiler_params=pltpu.CompilerParams(vmem_limit_bytes=40 * 1024 * 1024),
+    )(p)
 
 
 def mixed_dot(left, right):
     return jnp.dot(left, right, preferred_element_type=jnp.float32)
 
 
-def exact_dot(left, right):
-    return jnp.dot(left, right, precision=lax.Precision.HIGHEST, preferred_element_type=jnp.float32)
-
-
-def gram_of(power_all):
-    return mixed_dot(power_all.T, power_all)
+def two_pass(wide, narrow):
+    rows = wide.shape[0]
+    both = mixed_dot(jnp.concatenate(split(wide), 0), narrow)
+    return both[:rows] + both[rows:]
 
 
 def blocked_cholesky(grams):
@@ -43,9 +223,15 @@
     return jnp.concatenate([top, bottom], axis=1)
 
 
-def solve_rows(lower, power_rows):
-    solved = jax.scipy.linalg.solve_triangular(lower, power_rows.T.astype(jnp.float32), lower=True)
+def exact_orth(power):
+    lower = blocked_cholesky(mixed_dot(power.T, power)[None])[0]
+    solved = jax.scipy.linalg.solve_triangular(lower, power.T.astype(jnp.float32), lower=True)
     return solved.T.astype(jnp.bfloat16)
+
+
+def orthonormal(power):
+    quick, residual = orth(power)
+    return lax.cond(residual[0, 0] < RESIDUAL_LIMIT, lambda: quick, lambda: exact_orth(power))
 
 
 def per_device(
@@ -67,6 +253,7 @@
     row_count = left_factor.shape[2]
     block_width = features.shape[1]
     grad_scale = 1.0 / math.sqrt(features.shape[0] * owners)
+    core = lax.axis_index("fsdp") % 2
     first_row = lax.axis_index("fsdp") * row_count
     own_rows = lax.psum_scatter(
         mixed_dot(features.T, grad_rows) * grad_scale, "fsdp", scatter_dimension=0, tiled=True
@@ -91,29 +278,22 @@
     )
     power_left = mixed_dot(left_next.astype(jnp.bfloat16), left_old).astype(jnp.bfloat16)
     power_right = mixed_dot(right_next.astype(jnp.bfloat16), right_old).astype(jnp.bfloat16)
-    normed_all, power_left_all, power_right_all = (
-        lax.all_gather(normed, "fsdp", axis=0, tiled=True),
-        lax.all_gather(power_left, "fsdp", axis=0, tiled=True),
-        lax.all_gather(power_right, "fsdp", axis=0, tiled=True),
-    )
+    power_left_all = lax.all_gather(power_left, "fsdp", axis=0, tiled=True)
+    power_right_all = lax.all_gather(power_right, "fsdp", axis=0, tiled=True)
+    normed_all = lax.all_gather(normed, "fsdp", axis=0, tiled=True)
+    first_all = lax.all_gather(first_moment, "fsdp", axis=0, tiled=True)
+    mine = orthonormal(jnp.where(core == 0, power_left_all, power_right_all))
+    other = lax.ppermute(mine, "fsdp", [(d, d ^ 1) for d in range(owners)])
+    left_new = jnp.where(core == 0, mine, other)
+    right_new = jnp.where(core == 0, other, mine)
     left_rows = lax.dynamic_slice_in_dim(left_old, first_row, row_count, 0)
     back_half = mixed_dot(left_rows, normed_all).astype(jnp.bfloat16)
     update = mixed_dot(back_half, right_old.T)
-    lowers = blocked_cholesky(jnp.stack([gram_of(power_left_all), gram_of(power_right_all)]))
-    lower_left = lowers[0]
-    lower_right = lowers[1]
-    fresh_left = solve_rows(lower_left, power_left)
-    fresh_right = solve_rows(lower_right, power_right)
-    left_new, right_new = (
-        lax.all_gather(fresh_left, "fsdp", axis=0, tiled=True),
-        lax.all_gather(fresh_right, "fsdp", axis=0, tiled=True),
-    )
-    turn_right = mixed_dot(right_old.T, right_new)
-    carried_rows = exact_dot(first_moment, turn_right)
-    carried_all = lax.all_gather(carried_rows, "fsdp", axis=0, tiled=True)
     new_columns = lax.dynamic_slice_in_dim(left_new, first_row, row_count, 1)
     turn_rows = mixed_dot(new_columns.T, left_old)
-    moment_next = exact_dot(turn_rows, carried_all)
+    high_first, low_first = split(first_all)
+    moment_next = two_pass(turn_rows, high_first) + mixed_dot(turn_rows.astype(jnp.bfloat16), low_first)
+    moment_next = two_pass(two_pass(moment_next, right_old.T), right_new)
     island_delta = anchor[0] - (params[0, 0] - INNER_RATE * update)
     average = lax.psum(island_delta, "island") / lax.axis_size("island")
     momentum_next = OUTER_MOMENT * outer_momentum[0] + average

time: 1320 us -> 954 us (0.72)
  other arithmetic: 579 us -> 310 us
  waiting for transfers between devices: 516 us -> 424 us
  Pallas kernels: 0 us -> 23.5 us
  local copies, waits for them, and re-layouts: 87.3 us -> 66.1 us
    another operation x4 -> x3, other arithmetic: 162 us -> 81.3 us  [exact_orth(): jax.scipy.linalg.solve_triangular(lower, power.T.astype(jnp.float32), low...]
    another operation x16 -> x14, other arithmetic: 156 us -> 81.2 us  [blocked_cholesky(): head = jnp.linalg.cholesky(upper_left)]
    another operation x16 -> x15, other arithmetic: 157 us -> 89.4 us  [blocked_cholesky(): tail = jnp.linalg.cholesky(schur)]
    all_gather x6 -> x4, waiting for transfers between devices: 227 us -> 169 us  [the longest x1 61.4 us: per_device(): power_right_all = lax.all_gather(power_right, 'fsdp', axis=0, tiled=True)]
    another operation x3, other arithmetic: 83.9 us -> 42.3 us  [blocked_cholesky(): jax.scipy.linalg.solve_triangular(head, jnp.swapaxes(lower_left, 1, 2), l...]
    psum x1, waiting for transfers between devices: 35.8 us -> 0.01 us  [per_device(): average = lax.psum(island_delta, 'island') / lax.axis_size('island')]
    pallas_call x0 -> x1, Pallas kernels: none -> 23.5 us  [orth(): pl.pallas_call(orth_body, out_shape=(jax.ShapeDtypeStruct((N, N), bf), ja...]
    another operation x63 -> x38, local copies, waits for them, and re-layouts: 60.6 us -> 37.2 us  [the longest x51 46.2 us: solve_rows(): jax.scipy.linalg.solve_triangular(lower, power_rows.T.astype(jnp.float32)...]
  transfers between devices with their start and end apart: 10 -> 9, of which waited for: 8 -> 7; matrix products, arithmetic and copies ran while one was open for 57% -> 47% of each run, Pallas kernels for 0% -> 2%
where the time goes in v1:
time: 954 us; the launch traced here: 947 us
  waiting for transfers between devices  424 us (44%)
  other arithmetic  310 us (32%)
  matrix products  100 us (10%)
  local copies, waits for them, and re-layouts  66.1 us (7%)
  Pallas kernels  23.5 us (2%)
  between operations  15.2 us (2%)
    reduce_scatter x1, waiting for transfers between devices, per_device(): lax.psum_scatter(mixed_dot(features.T, grad_rows) * grad_scale, 'fsdp', s...  144 us
    another operation x15, other arithmetic, blocked_cholesky(): tail = jnp.linalg.cholesky(schur)  89.4 us
    another operation x3, other arithmetic, exact_orth(): jax.scipy.linalg.solve_triangular(lower, power.T.astype(jnp.float32), low...  81.3 us
    another operation x14, other arithmetic, blocked_cholesky(): head = jnp.linalg.cholesky(upper_left)  81.2 us
    all_gather x1, waiting for transfers between devices, per_device(): gradient_full = lax.all_gather(own_rows, 'fsdp', axis=0, tiled=True)  62.7 us
    all_gather x1, waiting for transfers between devices, per_device(): power_right_all = lax.all_gather(power_right, 'fsdp', axis=0, tiled=True)  61.4 us
    all_gather x1, waiting for transfers between devices, per_device(): power_left_all = lax.all_gather(power_left, 'fsdp', axis=0, tiled=True)  56.6 us
    all_gather x1, waiting for transfers between devices, per_device(): normed_all = lax.all_gather(normed, 'fsdp', axis=0, tiled=True)  50.6 us
  transfers between devices with their start and end apart: 9, of which 7 were waited for; matrix products, arithmetic and copies ran while one was open for 47% of the time, Pallas kernels for 2%

profile of v1, /device:TPU:32, one launch (start us, length us, event | category | flops | bytes accessed | tf_op | source)
XLA Modules:
  0.0 947.2 jit_solution(16511849240086872239)
XLA Ops:
  8.0 45.3 %all-gather.18.cloned.1.call-done = bf16[1,512,1024]{2,1,0:T(8,128)(2,1)} async-done(((bf16[1,512,512]{2,1,0:T(8,128)(2,1)}), bf16[1,512,1024]{2,1,0:T(8,128)(2,1)}) %all-gather.18.cloned.1.call-update) | async-done | bytes 1048592 | tf_op jit(solution)/shard_map/all_gather | solution.py:250
  53.2 4.8 convolution_multiply_fusion
  58.1 144.5 %reduce-scatter.2.cloned.1.call-done = f32[32,1024]{1,0:T(8,128)} async-done(((f32[1024,1024]{1,0:T(8,128)}), f32[32,1024]{1,0:T(8,128)}) %reduce-scatter.2.cloned.1.call-update) | async-done | bytes 131088 | tf_op jit(solution)/shard_map/reduce_scatter | solution.py:258
  204.3 62.7 %all-gather.8.cloned.1.call-done = bf16[1024,1024]{1,0:T(8,128)(2,1)} async-done(((bf16[32,1024]{1,0:T(8,128)(2,1)}), bf16[1024,1024]{1,0:T(8,128)(2,1)}) %all-gather.8.cloned.1.call-update) | async-done | bytes 2097168 | tf_op jit(solution)/shard_map/all_gather | solution.py:261
  266.9 4.0 fusion.148
  275.2 2.5 fusion.98
  279.5 50.6 %all-gather.10.cloned.1.call-done = bf16[1024,1024]{1,0:T(8,128)(2,1)} async-done(((bf16[32,1024]{1,0:T(8,128)(2,1)}), bf16[1024,1024]{1,0:T(8,128)(2,1)}) %all-gather.10.cloned.1.call-update) | async-done | bytes 2097168 | tf_op jit(solution)/shard_map/all_gather | solution.py:283
  330.2 4.0 fusion.105
  334.9 56.6 %all-gather.12.cloned.1.call-done = bf16[1024,1024]{1,0:T(8,128)(2,1)} async-done(((bf16[32,1024]{1,0:T(8,128)(2,1)}), bf16[1024,1024]{1,0:T(8,128)(2,1)}) %all-gather.12.cloned.1.call-update) | async-done | bytes 2097168 | tf_op jit(solution)/shard_map/all_gather | solution.py:281
  391.5 61.4 %all-gather.14.cloned.1.call-done = bf16[1024,1024]{1,0:T(8,128)(2,1)} async-done(((bf16[32,1024]{1,0:T(8,128)(2,1)}), bf16[1024,1024]{1,0:T(8,128)(2,1)}) %all-gather.14.cloned.1.call-update) | async-done | bytes 2097168 | tf_op jit(solution)/shard_map/all_gather | solution.py:282
  452.9 3.1 broadcast_select_fusion.2.p_ref
  456.0 23.5 %shard_map.170 = (bf16[1024,1024]{1,0:T(8,128)(2,1)}, f32[8,128]{1,0:T(8,128)S(1)}) custom-call(bf16[1024,1024]{1,0:T(8,128)(2,1)} %broadcast_select_fusion.2.p_ref), custom_call_target="tpu_custom_call" | custom-call | tf_op jit(solution)/shard_map/pallas_call | solution.py:187
  480.7 440.4 %conditional.1 = (bf16[1024,1024]{1,0:T(8,128)(2,1)}) conditional(s32[]{:T(128)} %bitcast.80, bf16[1024,1024]{1,0:T(8,128)(2,1)} %broadcast_select_fusion.2.p_ref, bf16[1024,1024]{1,0:T(8,128)(2,1)} %get-tuple-element.17), branch_computations={%region_2.12_spmd, %region_11.13_spmd} | conditional | flops 12836209664 | bytes 156968928 | solution.py:234
  480.9 4.7 convolution_bitcast_fusion
  492.3 11.7 %custom-call.39 = f32[1,128,128]{2,1,0:T(8,128)S(1)} custom-call(f32[1,128,128]{2,1,0:T(8,128)S(1)} %cholesky.425), custom_call_target="Cholesky" | custom-call | tf_op jit(solution)/shard_map/cond/branch_0_fun/jit(cholesky)/cholesky | solution.py:215
  504.2 9.8 %custom-call.40 = f32[1,1,128,128]{2,3,1,0:T(8,128)S(1)} custom-call(f32[1,1,128,128]{3,2,1,0:T(8,128)S(1)} %get-tuple-element.101), custom_call_target="InvertDiagBlocksLowerTriangular" | custom-call | tf_op jit(solution)/shard_map/cond/branch_0_fun/jit(cholesky)/cholesky | solution.py:215
  517.1 12.9 %custom-call.41 = f32[1,128,128]{2,1,0:T(8,128)S(1)} custom-call(f32[1,128,128]{2,1,0:T(8,128)} %cholesky.429), custom_call_target="Cholesky" | custom-call | tf_op jit(solution)/shard_map/cond/branch_0_fun/jit(cholesky)/cholesky | solution.py:215
  530.7 10.6 %custom-call.42 = f32[1,1,128,128]{2,3,1,0:T(8,128)S(1)} custom-call(f32[1,1,128,128]{3,2,1,0:T(8,128)} %get-tuple-element.98), custom_call_target="InvertDiagBlocksLowerTriangular" | custom-call | tf_op jit(solution)/shard_map/cond/branch_0_fun/jit(cholesky)/cholesky | solution.py:215
  542.9 11.7 %custom-call.43 = f32[1,128,128]{2,1,0:T(8,128)S(1)} custom-call(f32[1,128,128]{2,1,0:T(8,128)S(1)} %cholesky.434), custom_call_target="Cholesky" | custom-call | tf_op jit(solution)/shard_map/cond/branch_0_fun/jit(cholesky)/cholesky | solution.py:215
  554.7 9.8 %custom-call.44 = f32[1,1,128,128]{2,3,1,0:T(8,128)S(1)} custom-call(f32[1,1,128,128]{3,2,1,0:T(8,128)S(1)} %get-tuple-element.95), custom_call_target="InvertDiagBlocksLowerTriangular" | custom-call | tf_op jit(solution)/shard_map/cond/branch_0_fun/jit(cholesky)/cholesky | solution.py:215
  566.0 11.9 %custom-call.45 = f32[1,128,128]{2,1,0:T(8,128)S(1)} custom-call(f32[1,128,128]{2,1,0:T(8,128)S(1)} %fusion.32), custom_call_target="Cholesky" | custom-call | tf_op jit(solution)/shard_map/cond/branch_0_fun/jit(cholesky)/cholesky | solution.py:215
  584.0 14.2 %while.2 = (s32[]{:T(128)}, f32[512,512]{1,0:T(8,128)}, s32[4,2]{0,1:T(2,128)S(1)}, f32[4,128,128]{2,1,0:T(8,128)}, s32[]{:T(128)}) while((s32[]{:T(128)}, f32[512,512]{1,0:T(8,128)}, s32[4,2]{0,1:T(2,128)S(1)}, f32[4,128,128]{2,1,0:T(8,128)}, s32[]{:T(128)}) %tuple.88), condition=%wide.while_cond, body=%wide.while_body.sunk | while | flops 2 | bytes 132205 | solution.py:216
  584.7 2.9 bitcast_dynamic-update-slice_fusion.4
  588.2 2.9 bitcast_dynamic-update-slice_fusion.4
  591.8 2.9 bitcast_dynamic-update-slice_fusion.4
  595.3 2.8 bitcast_dynamic-update-slice_fusion.4
  598.1 40.7 %custom-call.30 = f32[4,128,128]{1,2,0:T(8,128)} custom-call(f32[4,128,128]{2,1,0:T(8,128)} %get-tuple-element.25), custom_call_target="InvertDiagBlocksLowerTriangular" | custom-call | tf_op jit(solution)/shard_map/cond/branch_0_fun/jit(_solve_triangular)/triangular_solve | solution.py:216
  651.5 3.6 fusion.16
  659.0 11.7 %custom-call.46 = f32[1,128,128]{2,1,0:T(8,128)S(1)} custom-call(f32[1,128,128]{2,1,0:T(8,128)S(1)} %cholesky.438), custom_call_target="Cholesky" | custom-call | tf_op jit(solution)/shard_map/cond/branch_0_fun/jit(cholesky)/cholesky | solution.py:219
  671.3 9.8 %custom-call.47 = f32[1,1,128,128]{2,3,1,0:T(8,128)S(1)} custom-call(f32[1,1,128,128]{3,2,1,0:T(8,128)S(1)} %get-tuple-element.91), custom_call_target="InvertDiagBlocksLowerTriangular" | custom-call | tf_op jit(solution)/shard_map/cond/branch_0_fun/jit(cholesky)/cholesky | solution.py:219
  685.2 12.3 %custom-call.48 = f32[1,128,128]{2,1,0:T(8,128)} custom-call(f32[1,128,128]{2,1,0:T(8,128)S(1)} %cholesky.442), custom_call_target="Cholesky" | custom-call | tf_op jit(solution)/shard_map/cond/branch_0_fun/jit(cholesky)/cholesky | solution.py:219
  700.9 11.3 %custom-call.49 = f32[1,1,128,128]{2,3,1,0:T(8,128)} custom-call(f32[1,1,128,128]{3,2,1,0:T(8,128)} %get-tuple-element.88), custom_call_target="InvertDiagBlocksLowerTriangular" | custom-call | tf_op jit(solution)/shard_map/cond/branch_0_fun/jit(cholesky)/cholesky | solution.py:219
  715.9 13.2 %custom-call.50 = f32[1,128,128]{2,1,0:T(8,128)} custom-call(f32[1,128,128]{2,1,0:T(8,128)} %cholesky.447), custom_call_target="Cholesky" | custom-call | tf_op jit(solution)/shard_map/cond/branch_0_fun/jit(cholesky)/cholesky | solution.py:219
  730.6 11.4 %custom-call.51 = f32[1,1,128,128]{2,3,1,0:T(8,128)} custom-call(f32[1,1,128,128]{3,2,1,0:T(8,128)} %get-tuple-element.85), custom_call_target="InvertDiagBlocksLowerTriangular" | custom-call | tf_op jit(solution)/shard_map/cond/branch_0_fun/jit(cholesky)/cholesky | solution.py:219
  744.9 13.2 %custom-call.52 = f32[1,128,128]{2,1,0:T(8,128)} custom-call(f32[1,128,128]{2,1,0:T(8,128)} %fusion.33), custom_call_target="Cholesky" | custom-call | tf_op jit(solution)/shard_map/cond/branch_0_fun/jit(cholesky)/cholesky | solution.py:219
  765.6 2.5 fusion.1
  768.1 23.2 %while.3 = (s32[]{:T(128)}, f32[1024,1024]{1,0:T(8,128)}, s32[8,2]{0,1:T(2,128)S(1)}, f32[8,128,128]{2,1,0:T(8,128)S(1)}, s32[]{:T(128)}) while((s32[]{:T(128)}, f32[1024,1024]{1,0:T(8,128)}, s32[8,2]{0,1:T(2,128)S(1)}, f32[8,128,128]{2,1,0:T(8,128)S(1)}, s32[]{:T(128)}) %tuple.91), condition=%wide.while_cond.1, body=%wide.while_body.1.sunk | while | flops 2 | bytes 131189 | solution.py:228
  791.3 78.8 %custom-call.31 = f32[8,128,128]{1,2,0:T(8,128)S(1)} custom-call(f32[8,128,128]{2,1,0:T(8,128)S(1)} %get-tuple-element.33), custom_call_target="InvertDiagBlocksLowerTriangular" | custom-call | tf_op jit(solution)/shard_map/cond/branch_0_fun/jit(_solve_triangular)/triangular_solve | solution.py:228
  877.5 2.7 convolution_subtract_fusion
  881.6 3.7 fusion.17
  886.7 4.5 fusion.20
  893.8 5.5 convolution_subtract_fusion.2
  900.8 6.1 convolution_subtract_fusion.1
  908.3 7.3 convolution_subtract_fusion.3
  917.0 4.0 copy.39
  923.2 2.6 collective-permute-done
  925.7 3.8 fusion.120
  931.5 2.8 fusion.118
  (201 shorter events, 116.8 us)
Async XLA Ops:
  7.2 259.8 %copy-start = (bf16[1,1,1024,1024]{3,2,1,0:T(8,128)(2,1)S(1)}, bf16[1,1,1024,1024]{3,2,1,0:T(8,128)(2,1)}, u32[]{:S(2)}) copy-start(bf16[1,1,1024,1024]{3,2,1,0:T(8,128)(2,1)} %param.20) | copy-start | bytes 6291460
  7.2 46.0 %all-gather.18.cloned.1.call-start = ((), (), s32[]{:S(2)}) async-start(), calls=%async_computation.8 | async-start | bytes 1572864 | tf_op jit(solution)/shard_map/all_gather | solution.py:250
  7.9 194.7 %reduce-scatter.2.cloned.1.call-start = ((), (), s32[]{:S(2)}) async-start(), calls=%async_computation.1 | async-start | bytes 4325376 | tf_op jit(solution)/shard_map/reduce_scatter | solution.py:258
  58.0 208.9 %copy-start.28 = (f32[1,1,32,1024]{3,2,1,0:T(8,128)S(1)}, f32[1,1,32,1024]{3,2,1,0:T(8,128)}, u32[]{:S(2)}) copy-start(f32[1,1,32,1024]{3,2,1,0:T(8,128)} %param.17) | copy-start | bytes 393220
  58.0 208.9 %copy-start.29 = (f32[1,1,32,1024]{3,2,1,0:T(8,128)S(1)}, f32[1,1,32,1024]{3,2,1,0:T(8,128)}, u32[]{:S(2)}) copy-start(f32[1,1,32,1024]{3,2,1,0:T(8,128)} %param.16) | copy-start | bytes 393220
  58.1 208.9 %all-gather.8.cloned.1.call-start = ((), (), s32[]{:S(2)}) async-start(), calls=%async_computation.2 | async-start | bytes 2162688 | tf_op jit(solution)/shard_map/all_gather | solution.py:261
  204.2 126.0 %all-gather.10.cloned.1.call-start = ((), (), s32[]{:S(2)}) async-start(), calls=%async_computation.3 | async-start | bytes 2162688 | tf_op jit(solution)/shard_map/all_gather | solution.py:283
  204.2 66.8 %copy-start.18 = (bf16[32,1024]{1,0:T(8,128)(2,1)S(1)}, bf16[32,1024]{1,0:T(8,128)(2,1)}, u32[]{:S(2)}) copy-start(bf16[32,1024]{1,0:T(8,128)(2,1)} %convert_element_type.74) | copy-start | bytes 196612
  204.2 66.8 %copy-start.25 = (f32[1,1,32,1024]{3,2,1,0:T(8,128)S(1)}, f32[1,1,32,1024]{3,2,1,0:T(8,128)}, u32[]{:S(2)}) copy-start(f32[1,1,32,1024]{3,2,1,0:T(8,128)} %param.18) | copy-start | bytes 393220
  270.9 4.3 copy-start.26
  271.0 120.6 %all-gather.12.cloned.1.call-start = ((), (), s32[]{:S(2)}) async-start(), calls=%async_computation.5 | async-start | bytes 2162688 | tf_op jit(solution)/shard_map/all_gather | solution.py:281
  273.4 0.7 copy-start.20
  275.1 55.0 %copy-start.19 = (f32[1,32,1024]{2,1,0:T(8,128)S(1)}, f32[1,32,1024]{2,1,0:T(8,128)}, u32[]{:S(2)}) copy-start(f32[1,32,1024]{2,1,0:T(8,128)} %param.23) | copy-start | bytes 393220
  275.2 55.0 %copy-start.27 = (f32[1,1,32,1024]{3,2,1,0:T(8,128)S(1)}, f32[1,1,32,1024]{3,2,1,0:T(8,128)}, u32[]{:S(2)}) copy-start(f32[1,1,32,1024]{3,2,1,0:T(8,128)} %param.22) | copy-start | bytes 393220
  275.2 177.7 %all-gather.14.cloned.1.call-start = ((), (), s32[]{:S(2)}) async-start(), calls=%async_computation.6 | async-start | bytes 2162688 | tf_op jit(solution)/shard_map/all_gather | solution.py:282
  275.2 3.1 copy-start.1
  277.7 0.7 copy-start.21
  279.5 642.0 %all-reduce.4.cloned.1.call-start = ((), (), s32[]{:S(2)}) async-start(), calls=%async_computation.4 | async-start | bytes 262144 | tf_op jit(solution)/shard_map/psum | solution.py:298
  334.2 597.4 %all-gather.16.cloned.1.call-start = ((), (), s32[]{:S(2)}) async-start(), calls=%async_computation.7 | async-start | bytes 4325376 | tf_op jit(solution)/shard_map/all_gather | solution.py:284
  485.6 2.7 copy-start.5
  491.3 1.0 copy-start.10
  584.0 59.0 %copy-start.7 = (f32[1,512,512]{2,1,0:T(8,128)S(1)}, f32[1,512,512]{2,1,0:T(8,128)}, u32[]{:S(2)}) copy-start(f32[1,512,512]{2,1,0:T(8,128)} %get-tuple-element.63) | copy-start | bytes 3145732 | tf_op jit(solution)/shard_map/cond
  638.9 5.5 copy-start.23
  643.0 3.5 copy-start.8
  644.9 1.7 copy-start.12
  657.9 1.0 copy-start.9
  670.7 0.6 copy-start.24
  682.6 1.9 copy-start.16
  684.5 0.7 copy-start.17
  714.7 0.7 copy-start.22
  764.2 1.0 copy-start.13
  764.2 1.0 copy-start.14
  764.2 1.1 copy-start.15
  764.2 1.4 copy-start.6
  921.1 4.6 collective-permute-start
  929.6 1.3 copy-start.11
  931.5 3.5 copy-start.3
  935.0 1.6 copy-start.2
  935.4 1.9 copy-start.4
Sparse Core Ops, SparseCore 0:
  9.8 43.3 all-gather.17
  58.2 144.3 reduce-scatter.1
  205.0 61.8 all-gather.7
  271.1 59.0 all-gather.9
  332.4 59.0 all-gather.11
  393.8 59.0 all-gather.13
  455.8 45.6 all-reduce.3
  504.0 63.5 all-gather.15

commit v2 on v1

--- a/solution.py
+++ b/solution.py
@@ -1,3 +1,4 @@
+import functools
 import math
 
 import jax
@@ -196,13 +197,211 @@
     )(p)
 
 
+WIDE = 640
+
+
+MESH_ID = pl.DeviceIdType.MESH
+
+
+def place():
+    f = lax.axis_index("fsdp")
+    return f // 8, (f // 2) % 4, f % 2
+
+
+def to_device(x, z, core):
+    return {"fsdp": (x * 4 + z) * 2 + core}
+
+
+def greet(peers):
+    barrier = pltpu.get_barrier_semaphore()
+    for peer in peers:
+        pl.semaphore_signal(barrier, inc=1, device_id=peer, device_id_type=MESH_ID)
+    pl.semaphore_wait(barrier, len(peers))
+
+
+def remote(src, dst, sends, recvs, index, peer):
+    return pltpu.make_async_remote_copy(
+        src_ref=src,
+        dst_ref=dst,
+        send_sem=sends.at[index],
+        recv_sem=recvs.at[index],
+        device_id=peer,
+        device_id_type=MESH_ID,
+    )
+
+
+def rows_at(start, count):
+    return pl.ds(pl.multiple_of(start, count), count)
+
+
+def start_all(copies):
+    for copy in copies:
+        copy.start()
+
+
+def wait_recv_all(copies):
+    for copy in copies:
+        copy.wait_recv()
+
+
+def gradient_body(scale, act, grads, lf, rf, g, fac, act2, flip, part, sent_c, got_c, sent_x, got_x, acc_x, sent_z, got_z, sent_f, twice, sends, recvs):
+    x, z, core = place()
+    tensor = lax.axis_index("tensor")
+    partner = to_device(x, z, 1 - core)
+    peers_x = [to_device((x + d) % 4, z, core) for d in (1, 2, 3)]
+    peers_z = [to_device(x, (z + d) % 4, core) for d in (1, 2, 3)]
+    other = {"tensor": 1 - tensor}
+    greet([partner, other] + peers_x + peers_z)
+    started = []
+
+    def launch(copies):
+        start_all(copies)
+        started.extend(copies)
+        return copies
+
+    swap = launch([remote(act, act2, sends, recvs, 0, other)])
+    chip = (x * 4 + z) * 64
+
+    near = pl.ds(pl.multiple_of(chip // 128 * 128, 128), WIDE)
+
+    def pack(factor):
+        narrow = factor[...].astype(jnp.bfloat16)
+        twice[:, :N] = narrow
+        twice[:, N:] = narrow
+        return twice[:, near]
+
+    @pl.when(core == 0)
+    def _():
+        fac[rows_at(chip, 32), :] = pack(lf)
+        sent_f[...] = pack(rf)
+
+    @pl.when(core == 1)
+    def _():
+        fac[rows_at(chip + 32, 32), :] = pack(rf)
+        sent_f[...] = pack(lf)
+
+    fac_c = launch([remote(sent_f, fac.at[rows_at(chip + core * 32, 32)], sends, recvs, 1, partner)])
+
+    def multiply(o, source):
+        flip[...] = source[...].T
+        sent_c[o] = nn(flip[rows_at((1 - core) * 256, 256), :], grads[...]).astype(jnp.bfloat16)
+        copies = launch([remote(sent_c.at[o], got_c.at[o], sends, recvs, 2 + o, partner)])
+        part[o] = nn(flip[rows_at(core * 256, 256), :], grads[...])
+        return copies
+
+    def reduce_x(o, copies):
+        wait_recv_all(copies)
+        part[o] += got_c[o].astype(jnp.float32)
+        for d in (1, 2, 3):
+            sent_x[o, d - 1] = part[o, rows_at((x + d) % 4 * 64, 64), :].astype(jnp.bfloat16)
+        return launch([
+            remote(sent_x.at[o, d], got_x.at[o, d], sends, recvs, 4 + o * 3 + d, peers_x[d]) for d in range(3)
+        ])
+
+    def reduce_z(o, copies):
+        wait_recv_all(copies)
+        total = part[o, rows_at(x * 64, 64), :]
+        for d in range(3):
+            total += got_x[o, d].astype(jnp.float32)
+        acc_x[o] = total
+        for d in (1, 2, 3):
+            sent_z[o, d - 1] = acc_x[o, rows_at((z + d) % 4 * 16, 16), :].astype(jnp.bfloat16)
+        return launch([
+            remote(sent_z.at[o, d], got_z.at[o, d], sends, recvs, 10 + o * 3 + d, peers_z[d]) for d in range(3)
+        ])
+
+    def base(o):
+        half = tensor if o == 0 else 1 - tensor
+        return half * 512 + core * 256
+
+    def gather_z(o, copies):
+        wait_recv_all(copies)
+        total = acc_x[o, rows_at(z * 16, 16), :]
+        for d in range(3):
+            total += got_z[o, d].astype(jnp.float32)
+        mine = rows_at(base(o) + x * 64 + z * 16, 16)
+        g[mine, :] = (total * scale).astype(jnp.bfloat16)
+        return launch([remote(g.at[mine], g.at[mine], sends, recvs, 16 + o * 3 + d, peers_z[d]) for d in range(3)])
+
+    def gather_x(o, copies):
+        wait_recv_all(copies)
+        mine = rows_at(base(o) + x * 64, 64)
+        return launch([remote(g.at[mine], g.at[mine], sends, recvs, 22 + o * 3 + d, peers_x[d]) for d in range(3)])
+
+    def gather_c(o, copies):
+        wait_recv_all(copies)
+        mine = rows_at(base(o), 256)
+        return launch([remote(g.at[mine], g.at[mine], sends, recvs, 28 + o, partner)])
+
+    c0 = multiply(0, act)
+    x0 = reduce_x(0, c0)
+    z0 = reduce_z(0, x0)
+    wait_recv_all(fac_c)
+    mine_z = rows_at(chip, 64)
+    fac_z = launch([remote(fac.at[mine_z], fac.at[mine_z], sends, recvs, 30 + d, peers_z[d]) for d in range(3)])
+    wait_recv_all(swap)
+    c1 = multiply(1, act2)
+    gz0 = gather_z(0, z0)
+    x1 = reduce_x(1, c1)
+    wait_recv_all(fac_z)
+    mine_x = rows_at(x * 256, 256)
+    fac_x = launch([remote(fac.at[mine_x], fac.at[mine_x], sends, recvs, 33 + d, peers_x[d]) for d in range(3)])
+    gx0 = gather_x(0, gz0)
+    z1 = reduce_z(1, x1)
+    gz1 = gather_z(1, z1)
+    gx1 = gather_x(1, gz1)
+    gc0 = gather_c(0, gx0)
+    gc1 = gather_c(1, gx1)
+    wait_recv_all(gc0)
+    wait_recv_all(fac_x)
+    wait_recv_all(gc1)
+    for copy in started:
+        copy.wait_send()
+
+
+def summed_gradient(activations, out_grads, lf, rf, scale):
+    bf, f32 = jnp.bfloat16, jnp.float32
+    vm = pl.BlockSpec(memory_space=pltpu.VMEM)
+    return pl.pallas_call(
+        functools.partial(gradient_body, scale),
+        out_shape=(jax.ShapeDtypeStruct((N, N), bf), jax.ShapeDtypeStruct((N, WIDE), bf)),
+        in_specs=[vm] * 4,
+        out_specs=(vm,) * 2,
+        scratch_shapes=[
+            pltpu.VMEM((512, 512), bf),
+            pltpu.VMEM((512, 512), bf),
+            pltpu.VMEM((2, 256, N), f32),
+            pltpu.VMEM((2, 256, N), bf),
+            pltpu.VMEM((2, 256, N), bf),
+            pltpu.VMEM((2, 3, 64, N), bf),
+            pltpu.VMEM((2, 3, 64, N), bf),
+            pltpu.VMEM((2, 64, N), f32),
+            pltpu.VMEM((2, 3, 16, N), bf),
+            pltpu.VMEM((2, 3, 16, N), bf),
+            pltpu.VMEM((32, WIDE), bf),
+            pltpu.VMEM((32, 2 * N), bf),
+            pltpu.SemaphoreType.DMA((36,)),
+            pltpu.SemaphoreType.DMA((36,)),
+        ],
+        compiler_params=pltpu.CompilerParams(
+            collective_id=0, has_side_effects=True, vmem_limit_bytes=40 * 1024 * 1024
+        ),
+        name="summed_gradient",
+    )(activations, out_grads, lf, rf)
+
+
 def mixed_dot(left, right):
     return jnp.dot(left, right, preferred_element_type=jnp.float32)
 
 
+def pair(x):
+    hi = lax.reduce_precision(x, 8, 7)
+    return hi.astype(jnp.bfloat16), (x - hi).astype(jnp.bfloat16)
+
+
 def two_pass(wide, narrow):
     rows = wide.shape[0]
-    both = mixed_dot(jnp.concatenate(split(wide), 0), narrow)
+    both = mixed_dot(jnp.concatenate(pair(wide), 0), narrow)
     return both[:rows] + both[rows:]
 
 
@@ -223,6 +422,17 @@
     return jnp.concatenate([top, bottom], axis=1)
 
 
+def whole_factor(near):
+    tiles = [[None] * 8 for _ in range(8)]
+    for b in range(8):
+        for k in range(5):
+            tile = near[b * 128:(b + 1) * 128, k * 128:(k + 1) * 128]
+            tiles[b][(b + k) % 8] = tile
+            if 0 < k < 4:
+                tiles[(b + k) % 8][b] = tile.T
+    return jnp.concatenate([jnp.concatenate(row, 1) for row in tiles], 0).astype(jnp.float32)
+
+
 def exact_orth(power):
     lower = blocked_cholesky(mixed_dot(power.T, power)[None])[0]
     solved = jax.scipy.linalg.solve_triangular(lower, power.T.astype(jnp.float32), lower=True)
@@ -247,18 +457,16 @@
     anchor,
     outer_momentum,
 ):
-    features = lax.all_gather(activations[0], "tensor", axis=1, tiled=True)
-    grad_rows = out_grads[0]
     owners = lax.axis_size("fsdp")
     row_count = left_factor.shape[2]
-    block_width = features.shape[1]
-    grad_scale = 1.0 / math.sqrt(features.shape[0] * owners)
+    block_width = left_factor.shape[3]
+    grad_scale = 1.0 / math.sqrt(activations.shape[1] * owners)
     core = lax.axis_index("fsdp") % 2
     first_row = lax.axis_index("fsdp") * row_count
-    own_rows = lax.psum_scatter(
-        mixed_dot(features.T, grad_rows) * grad_scale, "fsdp", scatter_dimension=0, tiled=True
-    ).astype(jnp.bfloat16)
-    gradient_full = lax.all_gather(own_rows, "fsdp", axis=0, tiled=True)
+    gradient_full, near_columns = summed_gradient(
+        activations[0], out_grads[0], left_factor[0, 0], right_factor[0, 0], grad_scale
+    )
+    own_rows = lax.dynamic_slice_in_dim(gradient_full, first_row, row_count, 0)
     left_old = left_basis[0, 0]
     right_old = right_basis[0, 0]
     left_columns = lax.dynamic_slice_in_dim(left_old, first_row, row_count, 1)
@@ -276,13 +484,17 @@
         FACTOR_BETA * right_factor[0, 0]
         + (1.0 - FACTOR_BETA) * mixed_dot(own_columns.T, gradient_full) / block_width
     )
-    power_left = mixed_dot(left_next.astype(jnp.bfloat16), left_old).astype(jnp.bfloat16)
-    power_right = mixed_dot(right_next.astype(jnp.bfloat16), right_old).astype(jnp.bfloat16)
-    power_left_all = lax.all_gather(power_left, "fsdp", axis=0, tiled=True)
-    power_right_all = lax.all_gather(power_right, "fsdp", axis=0, tiled=True)
+    oriented = jnp.where(core == 0, gradient_full, gradient_full.T)
+    factor_next = (
+        FACTOR_BETA * whole_factor(near_columns)
+        + (1.0 - FACTOR_BETA) * mixed_dot(oriented, oriented.T) / block_width
+    )
+    power = mixed_dot(
+        factor_next.astype(jnp.bfloat16), jnp.where(core == 0, left_old, right_old)
+    ).astype(jnp.bfloat16)
     normed_all = lax.all_gather(normed, "fsdp", axis=0, tiled=True)
     first_all = lax.all_gather(first_moment, "fsdp", axis=0, tiled=True)
-    mine = orthonormal(jnp.where(core == 0, power_left_all, power_right_all))
+    mine = orthonormal(power)
     other = lax.ppermute(mine, "fsdp", [(d, d ^ 1) for d in range(owners)])
     left_new = jnp.where(core == 0, mine, other)
     right_new = jnp.where(core == 0, other, mine)
@@ -291,7 +503,7 @@
     update = mixed_dot(back_half, right_old.T)
     new_columns = lax.dynamic_slice_in_dim(left_new, first_row, row_count, 1)
     turn_rows = mixed_dot(new_columns.T, left_old)
-    high_first, low_first = split(first_all)
+    high_first, low_first = pair(first_all)
     moment_next = two_pass(turn_rows, high_first) + mixed_dot(turn_rows.astype(jnp.bfloat16), low_first)
     moment_next = two_pass(two_pass(moment_next, right_old.T), right_new)
     island_delta = anchor[0] - (params[0, 0] - INNER_RATE * update)

time: 954 us -> 669 us (0.70)
  waiting for transfers between devices: 424 us -> 58.4 us
  Pallas kernels: 23.5 us -> 98.2 us
  local copies, waits for them, and re-layouts: 66.1 us -> 90.5 us
  other arithmetic: 310 us -> 296 us
    all_gather x4 -> x0, waiting for transfers between devices: 226 us -> none  [the longest x1 62.7 us: per_device(): gradient_full = lax.all_gather(own_rows, 'fsdp', axis=0, tiled=True)]
    reduce_scatter x1 -> x0, waiting for transfers between devices: 144 us -> none  [per_device(): lax.psum_scatter(mixed_dot(features.T, grad_rows) * grad_scale, 'fsdp', s...]
    pallas_call x0 -> x1, Pallas kernels: none -> 74.5 us  [summed_gradient(): pl.pallas_call(functools.partial(gradient_body, scale), out_shape=(jax.Sh...]
    unnamed x30 -> x54, local copies, waits for them, and re-layouts: 4.41 us -> 26 us
    another operation x15, other arithmetic: 89.4 us -> 79.2 us  [blocked_cholesky(): tail = jnp.linalg.cholesky(schur)]
    dot_general x13 -> x11, matrix products: 31.2 us -> 27.9 us  [mixed_dot(): return jnp.dot(left, right, preferred_element_type=jnp.float32)]
  transfers between devices with their start and end apart: 9 -> 4, of which waited for: 7 -> 2; matrix products, arithmetic and copies ran while one was open for 47% -> 69% of each run, Pallas kernels for 2% -> 4%
where the time goes in v2:
time: 669 us; the launch traced here: 661 us
  other arithmetic  296 us (44%)
  Pallas kernels  98.2 us (15%)
  matrix products  96.1 us (14%)
  local copies, waits for them, and re-layouts  90.5 us (14%)
  waiting for transfers between devices  58.4 us (9%)
  between operations  14.9 us (2%)
    another operation x3, other arithmetic, exact_orth(): jax.scipy.linalg.solve_triangular(lower, power.T.astype(jnp.float32), low...  81.5 us
    another operation x14, other arithmetic, blocked_cholesky(): head = jnp.linalg.cholesky(upper_left)  81 us
    another operation x15, other arithmetic, blocked_cholesky(): tail = jnp.linalg.cholesky(schur)  79.2 us
    pallas_call x1, Pallas kernels, summed_gradient(): pl.pallas_call(functools.partial(gradient_body, scale), out_shape=(jax.Sh...  74.5 us
    all_gather x1, waiting for transfers between devices, per_device(): normed_all = lax.all_gather(normed, 'fsdp', axis=0, tiled=True)  56.4 us
    another operation x15, matrix products, exact_orth(): jax.scipy.linalg.solve_triangular(lower, power.T.astype(jnp.float32), low...  43.6 us
    another operation x3, other arithmetic, blocked_cholesky(): jax.scipy.linalg.solve_triangular(head, jnp.swapaxes(lower_left, 1, 2), l...  42.4 us
    another operation x36, local copies, waits for them, and re-layouts  36.8 us
  transfers between devices with their start and end apart: 4, of which 2 were waited for; matrix products, arithmetic and copies ran while one was open for 69% of the time, Pallas kernels for 4%

profile of v2, /device:TPU:32, one launch (start us, length us, event | category | flops | bytes accessed | tf_op | source)
XLA Modules:
  0.0 661.0 jit_solution(7877907278254832238)
XLA Ops:
  11.3 74.5 %summed_gradient.1 = (bf16[1024,1024]{1,0:T(8,128)(2,1)S(1)}, bf16[1024,640]{1,0:T(8,128)(2,1)S(1)}) custom-call(bf16[512,512]{1,0:T(8,128)(2,1)S(1)} %bitcast.417, bf16[512,1024]{1,0:T(8,128)(2,1)S(1)} %bitcast.414, f32[32,1024]{1,0:T(8,128)S(1)} %bitcast.416, f32[32,1024]{1,0:T(8,128)S(1)} %bitcast.415), custom_call_target="tpu_custom_call" | custom-call | tf_op jit(solution)/shard_map/summed_gradient/pallas_call | solution.py:365
  85.8 3.5 fusion.147
  89.3 56.4 %all-gather.3.cloned.1.call-done = bf16[1024,1024]{1,0:T(8,128)(2,1)} async-done(((bf16[32,1024]{1,0:T(8,128)(2,1)}), bf16[1024,1024]{1,0:T(8,128)(2,1)}) %all-gather.3.cloned.1.call-update) | async-done | bytes 2097168 | tf_op jit(solution)/shard_map/all_gather | solution.py:495
  145.7 4.0 fusion.109
  156.7 2.5 copy.54
  178.3 10.0 %fusion.100.p_ref = bf16[1024,1024]{1,0:T(8,128)(2,1)} fusion(bf16[1,1,1024,1024]{3,2,1,0:T(8,128)(2,1)} %param.20, bf16[1,1,1024,1024]{3,2,1,0:T(8,128)(2,1)} %param.21, pred[]{:T(512)S(6)} %eq.4, bf16[1024,1024]{1,0:T(8,128)(2,1)} %slice_dynamic-update-slice_fusion.6, bf16[1024,1024]{1,0:T(8,128)(2,1)S(1)} %get-tuple-element.18, bf16[1024,1024]{0,1:T(8,128)(2,1)} %copy.54), kind=kOutput, calls=%fused_computation.229 | convolution fusion | flops 4303355904 | bytes 12582913 | tf_op jit(solution)/shard_map/dot_general | solution.py:394
  188.3 23.7 %shard_map.170 = (bf16[1024,1024]{1,0:T(8,128)(2,1)}, f32[8,128]{1,0:T(8,128)S(1)}) custom-call(bf16[1024,1024]{1,0:T(8,128)(2,1)} %fusion.100.p_ref), custom_call_target="tpu_custom_call" | custom-call | tf_op jit(solution)/shard_map/pallas_call | solution.py:188
  213.2 423.3 %conditional.1 = (bf16[1024,1024]{1,0:T(8,128)(2,1)}) conditional(s32[]{:T(128)} %bitcast.105, bf16[1024,1024]{1,0:T(8,128)(2,1)S(1)} %copy-done.8, bf16[1024,1024]{1,0:T(8,128)(2,1)} %get-tuple-element.21), branch_computations={%region_1.11_spmd, %region_10.12_spmd} | conditional | flops 12836209664 | bytes 176368064 | solution.py:444
  213.6 2.5 convolution_bitcast_fusion
  222.8 11.7 %custom-call.39 = f32[1,128,128]{2,1,0:T(8,128)S(1)} custom-call(f32[1,128,128]{2,1,0:T(8,128)S(1)} %cholesky.425), custom_call_target="Cholesky" | custom-call | tf_op jit(solution)/shard_map/cond/branch_0_fun/jit(cholesky)/cholesky | solution.py:414
  234.6 9.8 %custom-call.40 = f32[1,1,128,128]{2,3,1,0:T(8,128)S(1)} custom-call(f32[1,1,128,128]{3,2,1,0:T(8,128)S(1)} %get-tuple-element.99), custom_call_target="InvertDiagBlocksLowerTriangular" | custom-call | tf_op jit(solution)/shard_map/cond/branch_0_fun/jit(cholesky)/cholesky | solution.py:414
  247.0 12.5 %custom-call.41 = f32[1,128,128]{2,1,0:T(8,128)} custom-call(f32[1,128,128]{2,1,0:T(8,128)S(1)} %cholesky.429), custom_call_target="Cholesky" | custom-call | tf_op jit(solution)/shard_map/cond/branch_0_fun/jit(cholesky)/cholesky | solution.py:414
  262.4 10.4 %custom-call.42 = f32[1,1,128,128]{2,3,1,0:T(8,128)} custom-call(f32[1,1,128,128]{3,2,1,0:T(8,128)S(1)} %get-tuple-element.96), custom_call_target="InvertDiagBlocksLowerTriangular" | custom-call | tf_op jit(solution)/shard_map/cond/branch_0_fun/jit(cholesky)/cholesky | solution.py:414
  275.2 11.7 %custom-call.43 = f32[1,128,128]{2,1,0:T(8,128)S(1)} custom-call(f32[1,128,128]{2,1,0:T(8,128)S(1)} %cholesky.434), custom_call_target="Cholesky" | custom-call | tf_op jit(solution)/shard_map/cond/branch_0_fun/jit(cholesky)/cholesky | solution.py:414
  288.2 9.8 %custom-call.44 = f32[1,1,128,128]{2,3,1,0:T(8,128)S(1)} custom-call(f32[1,1,128,128]{3,2,1,0:T(8,128)S(1)} %get-tuple-element.93), custom_call_target="InvertDiagBlocksLowerTriangular" | custom-call | tf_op jit(solution)/shard_map/cond/branch_0_fun/jit(cholesky)/cholesky | solution.py:414
  299.5 12.1 %custom-call.45 = f32[1,128,128]{2,1,0:T(8,128)S(1)} custom-call(f32[1,128,128]{2,1,0:T(8,128)S(1)} %fusion.32), custom_call_target="Cholesky" | custom-call | tf_op jit(solution)/shard_map/cond/branch_0_fun/jit(cholesky)/cholesky | solution.py:414
  314.6 14.3 %while.2 = (s32[]{:T(128)}, f32[512,512]{1,0:T(8,128)}, s32[4,2]{0,1:T(2,128)S(1)}, f32[4,128,128]{2,1,0:T(8,128)}, s32[]{:T(128)}) while((s32[]{:T(128)}, f32[512,512]{1,0:T(8,128)}, s32[4,2]{0,1:T(2,128)S(1)}, f32[4,128,128]{2,1,0:T(8,128)}, s32[]{:T(128)}) %tuple.107), condition=%wide.while_cond, body=%wide.while_body.sunk | while | flops 2 | bytes 132705 | solution.py:415
  315.2 2.9 bitcast_dynamic-update-slice_fusion.4
  318.8 2.9 bitcast_dynamic-update-slice_fusion.4
  322.4 2.9 bitcast_dynamic-update-slice_fusion.4
  326.1 2.9 bitcast_dynamic-update-slice_fusion.4
  328.9 40.7 %custom-call.30 = f32[4,128,128]{1,2,0:T(8,128)} custom-call(f32[4,128,128]{2,1,0:T(8,128)} %get-tuple-element.29), custom_call_target="InvertDiagBlocksLowerTriangular" | custom-call | tf_op jit(solution)/shard_map/cond/branch_0_fun/jit(_solve_triangular)/triangular_solve | solution.py:415
  382.6 3.6 fusion.16
  390.1 11.7 %custom-call.46 = f32[1,128,128]{2,1,0:T(8,128)S(1)} custom-call(f32[1,128,128]{2,1,0:T(8,128)S(1)} %cholesky.438), custom_call_target="Cholesky" | custom-call | tf_op jit(solution)/shard_map/cond/branch_0_fun/jit(cholesky)/cholesky | solution.py:418
  401.9 9.8 %custom-call.47 = f32[1,1,128,128]{2,3,1,0:T(8,128)S(1)} custom-call(f32[1,1,128,128]{3,2,1,0:T(8,128)S(1)} %get-tuple-element.89), custom_call_target="InvertDiagBlocksLowerTriangular" | custom-call | tf_op jit(solution)/shard_map/cond/branch_0_fun/jit(cholesky)/cholesky | solution.py:418
  417.2 11.7 %custom-call.48 = f32[1,128,128]{2,1,0:T(8,128)S(1)} custom-call(f32[1,128,128]{2,1,0:T(8,128)S(1)} %cholesky.442), custom_call_target="Cholesky" | custom-call | tf_op jit(solution)/shard_map/cond/branch_0_fun/jit(cholesky)/cholesky | solution.py:418
  431.6 9.8 %custom-call.49 = f32[1,1,128,128]{2,3,1,0:T(8,128)S(1)} custom-call(f32[1,1,128,128]{3,2,1,0:T(8,128)S(1)} %get-tuple-element.86), custom_call_target="InvertDiagBlocksLowerTriangular" | custom-call | tf_op jit(solution)/shard_map/cond/branch_0_fun/jit(cholesky)/cholesky | solution.py:418
  443.9 11.7 %custom-call.50 = f32[1,128,128]{2,1,0:T(8,128)S(1)} custom-call(f32[1,128,128]{2,1,0:T(8,128)S(1)} %cholesky.447), custom_call_target="Cholesky" | custom-call | tf_op jit(solution)/shard_map/cond/branch_0_fun/jit(cholesky)/cholesky | solution.py:418
  456.9 10.0 %custom-call.51 = f32[1,1,128,128]{2,3,1,0:T(8,128)S(1)} custom-call(f32[1,1,128,128]{3,2,1,0:T(8,128)S(1)} %get-tuple-element.83), custom_call_target="InvertDiagBlocksLowerTriangular" | custom-call | tf_op jit(solution)/shard_map/cond/branch_0_fun/jit(cholesky)/cholesky | solution.py:418
  468.4 11.7 %custom-call.52 = f32[1,128,128]{2,1,0:T(8,128)S(1)} custom-call(f32[1,128,128]{2,1,0:T(8,128)S(1)} %fusion.33), custom_call_target="Cholesky" | custom-call | tf_op jit(solution)/shard_map/cond/branch_0_fun/jit(cholesky)/cholesky | solution.py:418
  483.0 2.5 fusion.1
  485.4 22.6 %while.3 = (s32[]{:T(128)}, f32[1024,1024]{1,0:T(8,128)}, s32[8,2]{0,1:T(2,128)S(1)}, f32[8,128,128]{2,1,0:T(8,128)S(1)}, s32[]{:T(128)}) while((s32[]{:T(128)}, f32[1024,1024]{1,0:T(8,128)}, s32[8,2]{0,1:T(2,128)S(1)}, f32[8,128,128]{2,1,0:T(8,128)S(1)}, s32[]{:T(128)}) %tuple.110), condition=%wide.while_cond.1, body=%wide.while_body.1.sunk | while | flops 2 | bytes 131181 | solution.py:438
  486.0 2.2 bitcast_dynamic-update-slice_fusion.5
  488.9 2.2 bitcast_dynamic-update-slice_fusion.5
  491.7 2.2 bitcast_dynamic-update-slice_fusion.5
  494.5 2.2 bitcast_dynamic-update-slice_fusion.5
  497.4 2.2 bitcast_dynamic-update-slice_fusion.5
  500.2 2.2 bitcast_dynamic-update-slice_fusion.5
  508.0 79.0 %custom-call.31 = f32[8,128,128]{1,2,0:T(8,128)S(1)} custom-call(f32[8,128,128]{2,1,0:T(8,128)S(1)} %get-tuple-element.37), custom_call_target="InvertDiagBlocksLowerTriangular" | custom-call | tf_op jit(solution)/shard_map/cond/branch_0_fun/jit(_solve_triangular)/triangular_solve | solution.py:438
  587.1 2.2 convert_dynamic-update-slice_fusion.6
  593.4 2.8 convolution_subtract_fusion
  597.7 3.7 fusion.17
  602.9 4.5 fusion.20
  609.1 5.4 convolution_subtract_fusion.2
  616.0 6.1 convolution_subtract_fusion.1
  623.6 7.3 %convolution_subtract_fusion.3 = f32[128,1024]{0,1:T(8,128)S(1)} fusion(f32[896,1024]{1,0:T(8,128)S(1)} %constant_dynamic-update-slice_fusion.11, f32[1024,1024]{0,1:T(8,128)S(1)} %bitcast_convert_fusion, f32[1024,1024]{1,0:T(8,128)} %get-tuple-element.249), kind=kOutput, calls=%fused_computation.31 | convolution fusion | flops 1409417216 | bytes 5177344 | tf_op jit(solution)/shard_map/cond/branch_0_fun/jit(_solve_triangular)/triangular_solve | solution.py:438
  632.3 4.0 copy.64
  646.6 2.8 fusion.87
  (220 shorter events, 118.5 us)
Async XLA Ops:
  7.2 138.6 %all-gather.3.cloned.1.call-start = ((), (), s32[]{:S(2)}) async-start(), calls=%async_computation | async-start | bytes 2162688 | tf_op jit(solution)/shard_map/all_gather | solution.py:495
  7.2 1.2 copy-start
  8.4 0.9 copy-start.1
  9.3 0.9 copy-start.3
  10.3 1.0 copy-start.5
  85.8 59.9 %copy-start.29 = (f32[1,32,1024]{2,1,0:T(8,128)S(1)}, f32[1,32,1024]{2,1,0:T(8,128)}, u32[]{:S(2)}) copy-start(f32[1,32,1024]{2,1,0:T(8,128)} %param.23) | copy-start | bytes 393220
  89.3 555.6 %all-reduce.4.cloned.1.call-start = ((), (), s32[]{:S(2)}) async-start(), calls=%async_computation.1 | async-start | bytes 262144 | tf_op jit(solution)/shard_map/psum | solution.py:510
  149.8 496.8 %all-gather.5.cloned.1.call-start = ((), (), s32[]{:S(2)}) async-start(), calls=%async_computation.2 | async-start | bytes 4325376 | tf_op jit(solution)/shard_map/all_gather | solution.py:496
  188.3 24.8 %copy-start.8 = (bf16[1024,1024]{1,0:T(8,128)(2,1)S(1)}, bf16[1024,1024]{1,0:T(8,128)(2,1)}, u32[]{:S(2)}) copy-start(bf16[1024,1024]{1,0:T(8,128)(2,1)} %fusion.100.p_ref) | copy-start | bytes 6291460
  213.2 423.7 %copy-start.2 = (f32[1,1,32,1024]{3,2,1,0:T(8,128)S(1)}, f32[1,1,32,1024]{3,2,1,0:T(8,128)}, u32[]{:S(2)}) copy-start(f32[1,1,32,1024]{3,2,1,0:T(8,128)} %param.19) | copy-start | bytes 393220
  213.6 2.5 copy-start.9
  216.1 2.7 copy-start.13
  221.8 1.0 copy-start.19
  314.5 59.2 %copy-start.16 = (f32[1,512,512]{2,1,0:T(8,128)S(1)}, f32[1,512,512]{2,1,0:T(8,128)}, u32[]{:S(2)}) copy-start(f32[1,512,512]{2,1,0:T(8,128)} %get-tuple-element.61) | copy-start | bytes 3145732 | tf_op jit(solution)/shard_map/cond
  369.6 5.5 copy-start.31
  373.7 3.5 copy-start.17
  375.6 1.7 copy-start.22
  379.0 1.3 copy-start.23
  380.2 0.7 copy-start.24
  380.9 0.7 copy-start.25
  389.0 1.0 copy-start.20
  416.5 0.7 copy-start.28
  481.4 1.2 copy-start.14
  481.4 1.5 copy-start.15
  587.0 2.4 copy-start.10
  636.5 1.6 copy-start.4
  636.5 4.5 copy-start.11
  636.5 4.5 collective-permute-start
  639.5 4.7 copy-start.18
  641.0 1.9 copy-start.26
  642.9 1.3 copy-start.21
  643.0 2.0 copy-start.30
  643.0 2.0 copy-start.32
  646.6 3.4 copy-start.7
  650.0 1.6 copy-start.6
  650.1 2.4 copy-start.27
  650.6 2.4 copy-start.12
Sparse Core Ops, SparseCore 0:
  89.4 56.2 all-gather.2
  149.9 45.5 all-reduce.3
  198.1 63.3 all-gather.4

commit v3 on v2

--- a/solution.py
+++ b/solution.py
@@ -128,73 +128,6 @@
     xh[...] = hi
     xl[...] = lo
     return left
-
-
-def orth_body(p_ref, q_ref, res_ref, pt, s_ref, a21, x_ref, sh, sl, xh, xl, l21h, l21l):
-    f, g = slice(0, H), slice(H, N)
-    a, b = slice(0, Q4), slice(Q4, H)
-    pt[...] = p_ref[...].T
-    s_ref[...] = nt(pt[f, :], pt[f, :])
-    a21[...] = nt(pt[g, :], pt[f, :])
-    r1 = leaf(s_ref, x_ref, sh, sl, xh, xl)
-
-    def by_x(t):
-        ta = tuple(v[:, a] for v in t)
-        xa, x2 = (xh[a, a], xl[a, a]), (xh[b, :], xl[b, :])
-        if len(t) == 1:
-            return nt(ta[0], xa[0]) + nt(ta[0], xa[1]), nt(t[0], x2[0]) + nt(t[0], x2[1])
-        return nt3(ta, xa), nt3(t, x2)
-
-    def l_rows(i, c):
-        rows = pl.ds(pl.multiple_of(i * Q4, Q4), Q4)
-        u, v = by_x(split(a21[rows, :]))
-        uh, ul = split(u)
-        vh, vl = split(v)
-        l21h[rows, a] = uh
-        l21h[rows, b] = vh
-        l21l[rows, a] = ul
-        l21l[rows, b] = vl
-        return c
-    lax.fori_loop(0, 2, l_rows, 0)
-
-    def q1_rows(i, c):
-        rows = pl.ds(pl.multiple_of(i * Q4, Q4), Q4)
-        u, v = by_x((p_ref[rows, f],))
-        uh, ul = split(u)
-        vh, vl = split(v)
-        q_ref[rows, a] = uh
-        q_ref[rows, Q4:H] = vh
-        pt[rows, a] = ul
-        pt[rows, Q4:H] = vl
-        return c
-
-    s_ref[...] = nt(pt[g, :], pt[g, :]) - nt3((l21h[...], l21l[...]), (l21h[...], l21l[...]))
-    lax.fori_loop(0, 4, q1_rows, 0)
-    r2 = leaf(s_ref, x_ref, sh, sl, xh, xl)
-
-    def q2_rows(i, c):
-        rows = pl.ds(pl.multiple_of(i * Q4, Q4), Q4)
-        t = p_ref[rows, g].astype(jnp.float32) - nt3((q_ref[rows, f], pt[rows, f]), (l21h[...], l21l[...]))
-        u, v = by_x(split(t))
-        q_ref[rows, H:H + Q4] = u.astype(jnp.bfloat16)
-        q_ref[rows, H + Q4:N] = v.astype(jnp.bfloat16)
-        return c
-    lax.fori_loop(0, 4, q2_rows, 0)
-    res_ref[...] = jnp.full((8, 128), jnp.maximum(r1, r2), jnp.float32)
-
-
-def orth(p):
-    bf, f32 = jnp.bfloat16, jnp.float32
-    return pl.pallas_call(
-        orth_body,
-        out_shape=(jax.ShapeDtypeStruct((N, N), bf), jax.ShapeDtypeStruct((8, 128), f32)),
-        in_specs=[pl.BlockSpec(memory_space=pltpu.VMEM)],
-        out_specs=(pl.BlockSpec(memory_space=pltpu.VMEM),) * 2,
-        scratch_shapes=[
-            pltpu.VMEM((N, N), bf), pltpu.VMEM((H, H), f32), pltpu.VMEM((H, H), f32), pltpu.VMEM((H, H), f32),
-        ] + [pltpu.VMEM((H, H), bf)] * 6,
-        compiler_params=pltpu.CompilerParams(vmem_limit_bytes=40 * 1024 * 1024),
-    )(p)
 
 
 WIDE = 640
@@ -390,6 +323,263 @@
     )(activations, out_grads, lf, rf)
 
 
+def refresh_body(
+    g, fac, lb, rb, mom, msq, lf, rf, par, anc, om,
+    left_out, right_out, p_own, p_other, first_all,
+    moment_out, msq_out, left_next, right_next, anchor_out, momentum_out, res_out,
+    turned, seen, out32, whole, gm, bo, p_ref, pt, q_ref, q_got, fx, keep, kept, upd, isl, mrows, res_own, res_got,
+    s_ref, a21, x_ref, sh, sl, xh, xl, l21h, l21l, sends, recvs, local,
+):
+    bf, f32 = jnp.bfloat16, jnp.float32
+    fsdp, island = lax.axis_index("fsdp"), lax.axis_index("island")
+    x, z, core = place()
+    partner = to_device(x, z, 1 - core)
+    peers_x = [to_device((x + d) % 4, z, core) for d in (1, 2, 3)]
+    peers_z = [to_device(x, (z + d) % 4, core) for d in (1, 2, 3)]
+    peers_y = [{"island": (island + d) % 4} for d in (1, 2, 3)]
+    chip = (x * 4 + z) * 64
+    f, h = slice(0, H), slice(H, N)
+    a, b = slice(0, Q4), slice(Q4, H)
+    greet([partner] + peers_x + peers_z + peers_y)
+    started = []
+
+    def launch(copies):
+        start_all(copies)
+        started.extend(copies)
+        return copies
+
+    def tile(i):
+        return rows_at(i * Q4, Q4)
+
+    turned[...] = lb[:, pl.ds(pl.multiple_of(fsdp // 4 * 128, 128), 128)].T
+    half = nn(turned[rows_at(fsdp % 4 * 32, 32), :], g[...]).astype(bf)
+    rotated = nn(half, rb[...])
+    first = BETA_ONE * mom[...] + (1.0 - BETA_ONE) * rotated
+    second = BETA_TWO * msq[...] + (1.0 - BETA_TWO) * rotated * rotated
+    msq_out[...] = second
+    normed = (first / (jnp.sqrt(second) + ADAM_EPS)).astype(bf)
+    first = first.astype(bf)
+
+    @pl.when(core == 0)
+    def _():
+        seen[rows_at(chip, 32), :] = normed
+        out32[...] = first
+        gm[...] = g[...]
+        bo[...] = lb[...]
+
+    @pl.when(core == 1)
+    def _():
+        seen[rows_at(chip + 32, 32), :] = first
+        out32[...] = normed
+        gm[...] = g[...].T
+        bo[...] = rb[...]
+
+    seen_c = launch([remote(out32, seen.at[rows_at(chip + core * 32, 32)], sends, recvs, 0, partner)])
+
+    for i in range(8):
+        for k in range(5):
+            j = (i + k) % 8
+            block = fac[i * 128:(i + 1) * 128, k * 128:(k + 1) * 128]
+            whole[i * 128:(i + 1) * 128, j * 128:(j + 1) * 128] = block
+            if 0 < k < 4:
+                whole[j * 128:(j + 1) * 128, i * 128:(i + 1) * 128] = block.T
+
+    wait_recv_all(seen_c)
+    mine = rows_at(chip, 64)
+    seen_z = launch([remote(seen.at[mine], seen.at[mine], sends, recvs, 1 + d, peers_z[d]) for d in range(3)])
+
+    def power_rows(i, c):
+        fx[...] = nt(gm[tile(i), :], gm[...]) * ((1.0 - FACTOR_BETA) / N)
+
+        @pl.when(i == x)
+        def _():
+            keep[...] = fx[rows_at(z * 64, 64), :]
+
+        nxt = (FACTOR_BETA * whole[tile(i), :].astype(f32) + fx[...]).astype(bf)
+        p_ref[tile(i), :] = nn(nxt, bo[...]).astype(bf)
+        return c
+
+    lax.fori_loop(0, 4, power_rows, 0)
+    p_copy = pltpu.make_async_copy(p_ref, p_own, local.at[0])
+    p_copy.start()
+    p_swap = launch([remote(p_ref, p_other, sends, recvs, 4, partner)])
+    away = rows_at((1 - core) * 32, 32)
+    kept_c = launch([remote(keep.at[away], kept, sends, recvs, 5, partner)])
+
+    pt[...] = p_ref[...].T
+    s_ref[...] = nt(pt[f, :], pt[f, :])
+    a21[...] = nt(pt[h, :], pt[f, :])
+    r1 = leaf(s_ref, x_ref, sh, sl, xh, xl)
+
+    wait_recv_all(seen_z)
+    mine = rows_at(x * 256, 256)
+    seen_x = launch([remote(seen.at[mine], seen.at[mine], sends, recvs, 6 + d, peers_x[d]) for d in range(3)])
+
+    def by_x(t):
+        ta = tuple(v[:, a] for v in t)
+        xa, x2 = (xh[a, a], xl[a, a]), (xh[b, :], xl[b, :])
+        if len(t) == 1:
+            return nt(ta[0], xa[0]) + nt(ta[0], xa[1]), nt(t[0], x2[0]) + nt(t[0], x2[1])
+        return nt3(ta, xa), nt3(t, x2)
+
+    def l_rows(i, c):
+        u, v = by_x(split(a21[tile(i), :]))
+        l21h[tile(i), a], l21l[tile(i), a] = split(u)
+        l21h[tile(i), b], l21l[tile(i), b] = split(v)
+        return c
+
+    lax.fori_loop(0, 2, l_rows, 0)
+    s_ref[...] = nt(pt[h, :], pt[h, :]) - nt3((l21h[...], l21l[...]), (l21h[...], l21l[...]))
+
+    def q1_rows(i, c):
+        u, v = by_x((p_ref[tile(i), f],))
+        q_ref[tile(i), a], pt[tile(i), a] = split(u)
+        q_ref[tile(i), b], pt[tile(i), b] = split(v)
+        return c
+
+    lax.fori_loop(0, 4, q1_rows, 0)
+    q1_swap = launch([remote(q_ref.at[:, pl.ds(0, H)], q_got.at[:, pl.ds(0, H)], sends, recvs, 9, partner)])
+
+    wait_recv_all(kept_c)
+    ours, theirs = keep[rows_at(core * 32, 32), :], kept[...]
+    left_next[...] = FACTOR_BETA * lf[...] + jnp.where(core == 0, ours, theirs)
+    right_next[...] = FACTOR_BETA * rf[...] + jnp.where(core == 0, theirs, ours)
+
+    r2 = leaf(s_ref, x_ref, sh, sl, xh, xl)
+    res_own[...] = jnp.full((8, 128), jnp.maximum(r1, r2), f32)
+    res_c = launch([remote(res_own, res_got, sends, recvs, 10, partner)])
+
+    wait_recv_all(seen_x)
+    upd_c = remote(upd.at[pl.ds(32, 32)], upd.at[pl.ds(32, 32)], sends, recvs, 11, partner)
+    first_copy = pltpu.make_async_copy(seen, first_all, local.at[1])
+    first_c = remote(seen, first_all, sends, recvs, 12, partner)
+
+    @pl.when(core == 0)
+    def _():
+        back = nn(lb[rows_at(chip, 64), :], seen[...]).astype(bf)
+        upd[...] = nt(back, rb[...])
+        upd_c.start()
+
+    @pl.when(core == 1)
+    def _():
+        first_copy.start()
+        first_c.start()
+
+    def q2_rows(i, c):
+        t = p_ref[tile(i), h].astype(f32) - nt3((q_ref[tile(i), f], pt[tile(i), f]), (l21h[...], l21l[...]))
+        u, v = by_x(split(t))
+        q_ref[tile(i), H:H + Q4] = u.astype(bf)
+        q_ref[tile(i), H + Q4:N] = v.astype(bf)
+        return c
+
+    lax.fori_loop(0, 4, q2_rows, 0)
+    q2_swap = launch([remote(q_ref.at[:, pl.ds(H, H)], q_got.at[:, pl.ds(H, H)], sends, recvs, 13, partner)])
+
+    @pl.when(core == 1)
+    def _():
+        upd_c.wait_recv()
+
+    delta = anc[...] - (par[...] - INNER_RATE * upd[rows_at(core * 32, 32), :])
+    isl[island] = delta
+    isl_y = launch([remote(isl.at[island], isl.at[island], sends, recvs, 14 + d, peers_y[d]) for d in range(3)])
+
+    wait_recv_all(q1_swap)
+    wait_recv_all(q2_swap)
+
+    def outs(flag):
+        left, right = (q_ref, q_got) if flag == 0 else (q_got, q_ref)
+        return [
+            pltpu.make_async_copy(left, left_out, local.at[2]),
+            pltpu.make_async_copy(right, right_out, local.at[3]),
+        ]
+
+    moment_c = remote(mrows.at[pl.ds(0, 32)], mrows.at[pl.ds(0, 32)], sends, recvs, 17, partner)
+
+    @pl.when(core == 0)
+    def _():
+        start_all(outs(0))
+
+    @pl.when(core == 1)
+    def _():
+        start_all(outs(1))
+
+        def twice(v, mm, m):
+            both = mm(jnp.concatenate(split(v), 0), m[...])
+            return both[:64] + both[64:]
+
+        turned[...] = q_got[:, pl.ds(pl.multiple_of(chip // 128 * 128, 128), 128)].T
+        turn = nn(turned[rows_at(chip % 128, 64), :], lb[...])
+        mrows[...] = twice(twice(twice(turn, nn, seen), nt, rb), nn, q_ref)
+        moment_c.start()
+
+    wait_recv_all(isl_y)
+    average = (isl[0] + isl[1] + isl[2] + isl[3]) / 4.0
+    momentum = OUTER_MOMENT * om[...] + average
+    momentum_out[...] = momentum
+    anchor_out[...] = anc[...] - OUTER_RATE * (average + OUTER_MOMENT * momentum)
+    wait_recv_all(res_c)
+    res_out[...] = jnp.maximum(res_own[...], res_got[...])
+    wait_recv_all(p_swap)
+    p_copy.wait()
+
+    @pl.when(core == 0)
+    def _():
+        first_c.wait_recv()
+        upd_c.wait_send()
+        moment_c.wait_recv()
+        for copy in outs(0):
+            copy.wait()
+
+    @pl.when(core == 1)
+    def _():
+        first_copy.wait()
+        first_c.wait_send()
+        moment_c.wait_send()
+        for copy in outs(1):
+            copy.wait()
+
+    moment_out[...] = mrows[rows_at(core * 32, 32), :]
+    for copy in started:
+        copy.wait_send()
+
+
+def refresh(gradient, near, left_old, right_old, rows):
+    bf, f32 = jnp.bfloat16, jnp.float32
+    vm, hbm = pl.BlockSpec(memory_space=pltpu.VMEM), pl.BlockSpec(memory_space=pl.ANY)
+    square = jax.ShapeDtypeStruct((N, N), bf)
+    strip = jax.ShapeDtypeStruct((32, N), f32)
+    big = pltpu.VMEM((N, N), bf)
+    return pl.pallas_call(
+        refresh_body,
+        out_shape=(square,) * 5 + (strip,) * 6 + (jax.ShapeDtypeStruct((8, 128), f32),),
+        in_specs=[vm] * 11,
+        out_specs=(hbm,) * 5 + (vm,) * 7,
+        scratch_shapes=[
+            pltpu.VMEM((128, N), bf),
+            big,
+            pltpu.VMEM((32, N), bf),
+            big, big, big, big, big, big, big,
+            pltpu.VMEM((Q4, N), f32),
+            pltpu.VMEM((64, N), f32),
+            pltpu.VMEM((32, N), f32),
+            pltpu.VMEM((64, N), f32),
+            pltpu.VMEM((4, 32, N), f32),
+            pltpu.VMEM((64, N), f32),
+            pltpu.VMEM((8, 128), f32),
+            pltpu.VMEM((8, 128), f32),
+            pltpu.VMEM((H, H), f32), pltpu.VMEM((H, H), f32), pltpu.VMEM((H, H), f32),
+        ] + [pltpu.VMEM((H, H), bf)] * 6 + [
+            pltpu.SemaphoreType.DMA((18,)),
+            pltpu.SemaphoreType.DMA((18,)),
+            pltpu.SemaphoreType.DMA((4,)),
+        ],
+        compiler_params=pltpu.CompilerParams(
+            collective_id=1, has_side_effects=True, vmem_limit_bytes=54 * 1024 * 1024
+        ),
+        name="refresh",
+    )(gradient, near, left_old, right_old, *rows)
+
+
 def mixed_dot(left, right):
     return jnp.dot(left, right, preferred_element_type=jnp.float32)
 
@@ -422,26 +612,10 @@
     return jnp.concatenate([top, bottom], axis=1)
 
 
-def whole_factor(near):
-    tiles = [[None] * 8 for _ in range(8)]
-    for b in range(8):
-        for k in range(5):
-            tile = near[b * 128:(b + 1) * 128, k * 128:(k + 1) * 128]
-            tiles[b][(b + k) % 8] = tile
-            if 0 < k < 4:
-                tiles[(b + k) % 8][b] = tile.T
-    return jnp.concatenate([jnp.concatenate(row, 1) for row in tiles], 0).astype(jnp.float32)
-
-
 def exact_orth(power):
     lower = blocked_cholesky(mixed_dot(power.T, power)[None])[0]
     solved = jax.scipy.linalg.solve_triangular(lower, power.T.astype(jnp.float32), lower=True)
     return solved.T.astype(jnp.bfloat16)
-
-
-def orthonormal(power):
-    quick, residual = orth(power)
-    return lax.cond(residual[0, 0] < RESIDUAL_LIMIT, lambda: quick, lambda: exact_orth(power))
 
 
 def per_device(
@@ -459,57 +633,29 @@
 ):
     owners = lax.axis_size("fsdp")
     row_count = left_factor.shape[2]
-    block_width = left_factor.shape[3]
     grad_scale = 1.0 / math.sqrt(activations.shape[1] * owners)
     core = lax.axis_index("fsdp") % 2
     first_row = lax.axis_index("fsdp") * row_count
-    gradient_full, near_columns = summed_gradient(
+    left_old, right_old = left_basis[0, 0], right_basis[0, 0]
+    gradient, near = summed_gradient(
         activations[0], out_grads[0], left_factor[0, 0], right_factor[0, 0], grad_scale
     )
-    own_rows = lax.dynamic_slice_in_dim(gradient_full, first_row, row_count, 0)
-    left_old = left_basis[0, 0]
-    right_old = right_basis[0, 0]
-    left_columns = lax.dynamic_slice_in_dim(left_old, first_row, row_count, 1)
-    half_turn = mixed_dot(left_columns.T, gradient_full).astype(jnp.bfloat16)
-    rotated = mixed_dot(half_turn, right_old)
-    first_moment = BETA_ONE * moment[0, 0] + (1.0 - BETA_ONE) * rotated
-    second_moment = BETA_TWO * moment_sq[0, 0] + (1.0 - BETA_TWO) * rotated * rotated
-    normed = (first_moment / (jnp.sqrt(second_moment) + ADAM_EPS)).astype(jnp.bfloat16)
-    own_columns = lax.dynamic_slice_in_dim(gradient_full, first_row, row_count, 1)
-    left_next = (
-        FACTOR_BETA * left_factor[0, 0]
-        + (1.0 - FACTOR_BETA) * mixed_dot(own_rows, gradient_full.T) / block_width
-    )
-    right_next = (
-        FACTOR_BETA * right_factor[0, 0]
-        + (1.0 - FACTOR_BETA) * mixed_dot(own_columns.T, gradient_full) / block_width
-    )
-    oriented = jnp.where(core == 0, gradient_full, gradient_full.T)
-    factor_next = (
-        FACTOR_BETA * whole_factor(near_columns)
-        + (1.0 - FACTOR_BETA) * mixed_dot(oriented, oriented.T) / block_width
-    )
-    power = mixed_dot(
-        factor_next.astype(jnp.bfloat16), jnp.where(core == 0, left_old, right_old)
-    ).astype(jnp.bfloat16)
-    normed_all = lax.all_gather(normed, "fsdp", axis=0, tiled=True)
-    first_all = lax.all_gather(first_moment, "fsdp", axis=0, tiled=True)
-    mine = orthonormal(power)
-    other = lax.ppermute(mine, "fsdp", [(d, d ^ 1) for d in range(owners)])
-    left_new = jnp.where(core == 0, mine, other)
-    right_new = jnp.where(core == 0, other, mine)
-    left_rows = lax.dynamic_slice_in_dim(left_old, first_row, row_count, 0)
-    back_half = mixed_dot(left_rows, normed_all).astype(jnp.bfloat16)
-    update = mixed_dot(back_half, right_old.T)
-    new_columns = lax.dynamic_slice_in_dim(left_new, first_row, row_count, 1)
-    turn_rows = mixed_dot(new_columns.T, left_old)
-    high_first, low_first = pair(first_all)
-    moment_next = two_pass(turn_rows, high_first) + mixed_dot(turn_rows.astype(jnp.bfloat16), low_first)
-    moment_next = two_pass(two_pass(moment_next, right_old.T), right_new)
-    island_delta = anchor[0] - (params[0, 0] - INNER_RATE * update)
-    average = lax.psum(island_delta, "island") / lax.axis_size("island")
-    momentum_next = OUTER_MOMENT * outer_momentum[0] + average
-    anchor_next = anchor[0] - OUTER_RATE * (average + OUTER_MOMENT * momentum_next)
+    rows = (moment, moment_sq, left_factor, right_factor, params)
+    rows = tuple(v[0, 0] for v in rows) + (anchor[0], outer_momentum[0])
+    (
+        left_quick, right_quick, power, power_other, first_all,
+        moment_quick, second_moment, left_next, right_next, anchor_next, momentum_next, residual,
+    ) = refresh(gradient, near, left_old, right_old, rows)
+
+    def redo(state):
+        left_new = exact_orth(jnp.where(core == 0, power, power_other))
+        right_new = exact_orth(jnp.where(core == 0, power_other, power))
+        new_columns = lax.dynamic_slice_in_dim(left_new, first_row, row_count, 1)
+        turned = two_pass(mixed_dot(new_columns.T, left_old), first_all)
+        return False, left_new, right_new, two_pass(two_pass(turned, right_old.T), right_new)
+
+    quick = (jnp.logical_not(residual[0, 0] < RESIDUAL_LIMIT), left_quick, right_quick, moment_quick)
+    _, left_new, right_new, moment_next = lax.while_loop(lambda state: state[0], redo, quick)
     return (
         anchor_next[None],
         momentum_next[None],

time: 669 us -> 971 us (1.45)
  other arithmetic: 296 us -> 571 us
  waiting for transfers between devices: 58.4 us -> 0 us
  Pallas kernels: 98.2 us -> 135 us
  matrix products: 96.1 us -> 129 us
  local copies, waits for them, and re-layouts: 90.5 us -> 111 us
  between operations: 14.9 us -> 1.71 us
  loops' own time: 6.63 us -> 17 us
    another operation x3 -> x5, other arithmetic: 81.5 us -> 163 us  [exact_orth(): jax.scipy.linalg.solve_triangular(lower, power.T.astype(jnp.float32), low...]
    another operation x14 -> x30, other arithmetic: 81 us -> 159 us  [blocked_cholesky(): head = jnp.linalg.cholesky(upper_left)]
    another operation x15 -> x26, other arithmetic: 79.2 us -> 156 us  [blocked_cholesky(): tail = jnp.linalg.cholesky(schur)]
    all_gather x2 -> x0, waiting for transfers between devices: 56.4 us -> none  [the longest x1 56.4 us: per_device(): normed_all = lax.all_gather(normed, 'fsdp', axis=0, tiled=True)]
    another operation x2 -> x51, local copies, waits for them, and re-layouts: 0.05 us -> 46.2 us  [exact_orth(): jax.scipy.linalg.solve_triangular(lower, power.T.astype(jnp.float32), low...]
    another operation x3 -> x5, other arithmetic: 42.4 us -> 81.3 us  [blocked_cholesky(): jax.scipy.linalg.solve_triangular(head, jnp.swapaxes(lower_left, 1, 2), l...]
    another operation x36 -> x0, local copies, waits for them, and re-layouts: 36.8 us -> none
    pallas_call x1, Pallas kernels: 23.7 us -> 60.3 us  [refresh(): pl.pallas_call(refresh_body, out_shape=(square,) * 5 + (strip,) * 6 + (ja...]
  transfers between devices with their start and end apart: 4 -> 0, of which waited for: 2 -> 0; matrix products, arithmetic and copies ran while one was open for 69% -> 0% of each run, Pallas kernels for 4% -> 0%
where the time goes in v3:
time: 971 us; the launch traced here: 965 us
  other arithmetic  571 us (59%)
  Pallas kernels  135 us (14%)
  matrix products  129 us (13%)
  local copies, waits for them, and re-layouts  111 us (11%)
  loops' own time  17 us (2%)
    another operation x5, other arithmetic, exact_orth(): jax.scipy.linalg.solve_triangular(lower, power.T.astype(jnp.float32), low...  163 us
    another operation x30, other arithmetic, blocked_cholesky(): head = jnp.linalg.cholesky(upper_left)  159 us
    another operation x26, other arithmetic, blocked_cholesky(): tail = jnp.linalg.cholesky(schur)  156 us
    another operation x5, other arithmetic, blocked_cholesky(): jax.scipy.linalg.solve_triangular(head, jnp.swapaxes(lower_left, 1, 2), l...  81.3 us
    another operation x30, matrix products, exact_orth(): jax.scipy.linalg.solve_triangular(lower, power.T.astype(jnp.float32), low...  76.5 us
    pallas_call x1, Pallas kernels, summed_gradient(): pl.pallas_call(functools.partial(gradient_body, scale), out_shape=(jax.Sh...  74.5 us
    pallas_call x1, Pallas kernels, refresh(): pl.pallas_call(refresh_body, out_shape=(square,) * 5 + (strip,) * 6 + (ja...  60.3 us
    another operation x51, local copies, waits for them, and re-layouts, exact_orth(): jax.scipy.linalg.solve_triangular(lower, power.T.astype(jnp.float32), low...  46.2 us

profile of v3, /device:TPU:32, one launch (start us, length us, event | category | flops | bytes accessed | tf_op | source)
XLA Modules:
  0.0 964.7 jit_solution(9082209295775281096)
XLA Ops:
  4.7 74.5 %summed_gradient.1 = (bf16[1024,1024]{1,0:T(8,128)(2,1)S(1)}, bf16[1024,640]{1,0:T(8,128)(2,1)S(1)}) custom-call(bf16[512,512]{1,0:T(8,128)(2,1)S(1)} %bitcast.533, bf16[512,1024]{1,0:T(8,128)(2,1)S(1)} %bitcast.528, f32[32,1024]{1,0:T(8,128)S(1)} %bitcast.530, f32[32,1024]{1,0:T(8,128)S(1)} %bitcast.532), custom_call_target="tpu_custom_call" | custom-call | tf_op jit(solution)/shard_map/summed_gradient/pallas_call | solution.py:298
  81.6 60.3 %refresh.1 = (bf16[1024,1024]{1,0:T(8,128)(2,1)}, bf16[1024,1024]{1,0:T(8,128)(2,1)}, bf16[1024,1024]{1,0:T(8,128)(2,1)}, bf16[1024,1024]{1,0:T(8,128)(2,1)}, bf...) custom-call(bf16[1024,1024]{1,0:T(8,128)(2,1)} %copy-done, ...), custom_call_target="tpu_custom_call" | custom-call | tf_op jit(solution)/shard_map/refresh/pallas_call | solution.py:552
  150.4 803.3 %while.13 = (pred[]{:T(512)}, bf16[1024,1024]{0,1:T(8,128)(2,1)}, bf16[1024,1024]{0,1:T(8,128)(2,1)}, f32[32,1024]{1,0:T(8,128)}, s32[]{:T(128)}, /*index=5*/bf1...) while((pred[]{:T(512)}, bf16[1024,1024]{0,1:T(8,128)(2,1)}, ...), condition=%region_9.13_spmd, body=%region_0.12_spmd | while | flops 26145556480 | bytes 334841376 | solution.py:658
  150.8 4.7 convolution_bitcast_fusion.1
  159.5 11.7 %custom-call.53 = f32[1,128,128]{2,1,0:T(8,128)S(1)} custom-call(f32[1,128,128]{2,1,0:T(8,128)S(1)} %cholesky.741), custom_call_target="Cholesky" | custom-call | tf_op jit(solution)/shard_map/while/body/jit(cholesky)/cholesky | solution.py:604
  171.2 9.8 %custom-call.54 = f32[1,1,128,128]{2,3,1,0:T(8,128)S(1)} custom-call(f32[1,1,128,128]{3,2,1,0:T(8,128)S(1)} %get-tuple-element.307), custom_call_target="InvertDiagBlocksLowerTriangular" | custom-call | tf_op jit(solution)/shard_map/while/body/jit(cholesky)/cholesky | solution.py:604
  181.8 11.9 %custom-call.55 = f32[1,128,128]{2,1,0:T(8,128)S(1)} custom-call(f32[1,128,128]{2,1,0:T(8,128)S(1)} %cholesky.745), custom_call_target="Cholesky" | custom-call | tf_op jit(solution)/shard_map/while/body/jit(cholesky)/cholesky | solution.py:604
  193.7 9.8 %custom-call.56 = f32[1,1,128,128]{2,3,1,0:T(8,128)S(1)} custom-call(f32[1,1,128,128]{3,2,1,0:T(8,128)S(1)} %get-tuple-element.304), custom_call_target="InvertDiagBlocksLowerTriangular" | custom-call | tf_op jit(solution)/shard_map/while/body/jit(cholesky)/cholesky | solution.py:604
  204.2 11.7 %custom-call.57 = f32[1,128,128]{2,1,0:T(8,128)S(1)} custom-call(f32[1,128,128]{2,1,0:T(8,128)S(1)} %cholesky.750), custom_call_target="Cholesky" | custom-call | tf_op jit(solution)/shard_map/while/body/jit(cholesky)/cholesky | solution.py:604
  219.8 9.8 %custom-call.58 = f32[1,1,128,128]{2,3,1,0:T(8,128)S(1)} custom-call(f32[1,1,128,128]{3,2,1,0:T(8,128)S(1)} %get-tuple-element.301), custom_call_target="InvertDiagBlocksLowerTriangular" | custom-call | tf_op jit(solution)/shard_map/while/body/jit(cholesky)/cholesky | solution.py:604
  230.2 12.1 %custom-call.59 = f32[1,128,128]{2,1,0:T(8,128)S(1)} custom-call(f32[1,128,128]{2,1,0:T(8,128)S(1)} %fusion.62), custom_call_target="Cholesky" | custom-call | tf_op jit(solution)/shard_map/while/body/jit(cholesky)/cholesky | solution.py:604
  244.9 11.6 %while.22 = (s32[]{:T(128)}, f32[512,512]{1,0:T(8,128)}, s32[4,2]{0,1:T(2,128)S(1)}, f32[4,128,128]{2,1,0:T(8,128)S(1)}, s32[]{:T(128)}) while((s32[]{:T(128)}, f32[512,512]{1,0:T(8,128)}, s32[4,2]{0,1:T(2,128)S(1)}, f32[4,128,128]{2,1,0:T(8,128)S(1)}, s32[]{:T(128)}) %tuple.161), condition=%wide.while_cond, body=%wide.while_body.sunk | while | flops 2 | bytes 131181 | solution.py:605
  256.5 39.3 %custom-call.60 = f32[4,128,128]{1,2,0:T(8,128)S(1)} custom-call(f32[4,128,128]{2,1,0:T(8,128)S(1)} %get-tuple-element.125), custom_call_target="InvertDiagBlocksLowerTriangular" | custom-call | tf_op jit(solution)/shard_map/while/body/jit(_solve_triangular)/triangular_solve | solution.py:605
  311.8 11.7 %custom-call.61 = f32[1,128,128]{2,1,0:T(8,128)S(1)} custom-call(f32[1,128,128]{2,1,0:T(8,128)S(1)} %cholesky.754), custom_call_target="Cholesky" | custom-call | tf_op jit(solution)/shard_map/while/body/jit(cholesky)/cholesky | solution.py:608
  323.7 9.8 %custom-call.62 = f32[1,1,128,128]{2,3,1,0:T(8,128)S(1)} custom-call(f32[1,1,128,128]{3,2,1,0:T(8,128)S(1)} %get-tuple-element.297), custom_call_target="InvertDiagBlocksLowerTriangular" | custom-call | tf_op jit(solution)/shard_map/while/body/jit(cholesky)/cholesky | solution.py:608
  337.3 11.7 %custom-call.63 = f32[1,128,128]{2,1,0:T(8,128)S(1)} custom-call(f32[1,128,128]{2,1,0:T(8,128)S(1)} %cholesky.758), custom_call_target="Cholesky" | custom-call | tf_op jit(solution)/shard_map/while/body/jit(cholesky)/cholesky | solution.py:608
  349.0 9.8 %custom-call.64 = f32[1,1,128,128]{2,3,1,0:T(8,128)S(1)} custom-call(f32[1,1,128,128]{3,2,1,0:T(8,128)S(1)} %get-tuple-element.294), custom_call_target="InvertDiagBlocksLowerTriangular" | custom-call | tf_op jit(solution)/shard_map/while/body/jit(cholesky)/cholesky | solution.py:608
  361.3 11.7 %custom-call.65 = f32[1,128,128]{2,1,0:T(8,128)S(1)} custom-call(f32[1,128,128]{2,1,0:T(8,128)S(1)} %cholesky.763), custom_call_target="Cholesky" | custom-call | tf_op jit(solution)/shard_map/while/body/jit(cholesky)/cholesky | solution.py:608
  373.1 10.0 %custom-call.66 = f32[1,1,128,128]{2,3,1,0:T(8,128)S(1)} custom-call(f32[1,1,128,128]{3,2,1,0:T(8,128)S(1)} %get-tuple-element.291), custom_call_target="InvertDiagBlocksLowerTriangular" | custom-call | tf_op jit(solution)/shard_map/while/body/jit(cholesky)/cholesky | solution.py:608
  384.5 11.7 %custom-call.67 = f32[1,128,128]{2,1,0:T(8,128)S(1)} custom-call(f32[1,128,128]{2,1,0:T(8,128)S(1)} %fusion.63), custom_call_target="Cholesky" | custom-call | tf_op jit(solution)/shard_map/while/body/jit(cholesky)/cholesky | solution.py:608
  402.8 23.2 %while.23 = (s32[]{:T(128)}, f32[1024,1024]{1,0:T(8,128)}, s32[8,2]{0,1:T(2,128)S(1)}, f32[8,128,128]{2,1,0:T(8,128)S(1)}, s32[]{:T(128)}) while((s32[]{:T(128)}, f32[1024,1024]{1,0:T(8,128)}, s32[8,2]{0,1:T(2,128)S(1)}, f32[8,128,128]{2,1,0:T(8,128)S(1)}, s32[]{:T(128)}) %tuple.164), condition=%wide.while_cond.1, body=%wide.while_body.1.sunk | while | flops 2 | bytes 131181 | solution.py:617
  426.0 79.0 %custom-call.68 = f32[8,128,128]{1,2,0:T(8,128)S(1)} custom-call(f32[8,128,128]{2,1,0:T(8,128)S(1)} %get-tuple-element.126), custom_call_target="InvertDiagBlocksLowerTriangular" | custom-call | tf_op jit(solution)/shard_map/while/body/jit(_solve_triangular)/triangular_solve | solution.py:617
  505.0 4.7 convert_bitcast_fusion
  526.3 5.4 convolution_subtract_fusion.5
  532.4 6.2 convolution_subtract_fusion.3
  539.2 7.5 convolution_subtract_fusion.8
  553.7 4.7 convolution_bitcast_fusion
  562.4 12.1 %custom-call.69 = f32[1,128,128]{2,1,0:T(8,128)S(1)} custom-call(f32[1,128,128]{2,1,0:T(8,128)S(1)} %cholesky.767), custom_call_target="Cholesky" | custom-call | tf_op jit(solution)/shard_map/while/body/jit(cholesky)/cholesky | solution.py:604
  574.5 9.8 %custom-call.70 = f32[1,1,128,128]{2,3,1,0:T(8,128)S(1)} custom-call(f32[1,1,128,128]{3,2,1,0:T(8,128)S(1)} %get-tuple-element.287), custom_call_target="InvertDiagBlocksLowerTriangular" | custom-call | tf_op jit(solution)/shard_map/while/body/jit(cholesky)/cholesky | solution.py:604
  585.1 11.7 %custom-call.71 = f32[1,128,128]{2,1,0:T(8,128)S(1)} custom-call(f32[1,128,128]{2,1,0:T(8,128)S(1)} %cholesky.771), custom_call_target="Cholesky" | custom-call | tf_op jit(solution)/shard_map/while/body/jit(cholesky)/cholesky | solution.py:604
  596.9 9.8 %custom-call.72 = f32[1,1,128,128]{2,3,1,0:T(8,128)S(1)} custom-call(f32[1,1,128,128]{3,2,1,0:T(8,128)S(1)} %get-tuple-element.284), custom_call_target="InvertDiagBlocksLowerTriangular" | custom-call | tf_op jit(solution)/shard_map/while/body/jit(cholesky)/cholesky | solution.py:604
  607.4 11.9 %custom-call.73 = f32[1,128,128]{2,1,0:T(8,128)S(1)} custom-call(f32[1,128,128]{2,1,0:T(8,128)S(1)} %cholesky.776), custom_call_target="Cholesky" | custom-call | tf_op jit(solution)/shard_map/while/body/jit(cholesky)/cholesky | solution.py:604
  623.2 9.8 %custom-call.74 = f32[1,1,128,128]{2,3,1,0:T(8,128)S(1)} custom-call(f32[1,1,128,128]{3,2,1,0:T(8,128)S(1)} %get-tuple-element.281), custom_call_target="InvertDiagBlocksLowerTriangular" | custom-call | tf_op jit(solution)/shard_map/while/body/jit(cholesky)/cholesky | solution.py:604
  633.6 11.7 %custom-call.75 = f32[1,128,128]{2,1,0:T(8,128)S(1)} custom-call(f32[1,128,128]{2,1,0:T(8,128)S(1)} %fusion.64), custom_call_target="Cholesky" | custom-call | tf_op jit(solution)/shard_map/while/body/jit(cholesky)/cholesky | solution.py:604
  647.9 12.0 %while.24 = (s32[]{:T(128)}, f32[512,512]{1,0:T(8,128)}, s32[4,2]{0,1:T(2,128)S(1)}, f32[4,128,128]{2,1,0:T(8,128)S(1)}, s32[]{:T(128)}) while((s32[]{:T(128)}, f32[512,512]{1,0:T(8,128)}, s32[4,2]{0,1:T(2,128)S(1)}, f32[4,128,128]{2,1,0:T(8,128)S(1)}, s32[]{:T(128)}) %tuple.180), condition=%wide.while_cond.clone, body=%wide.while_body.clone.sunk | while | flops 2 | bytes 131181 | solution.py:605
  659.9 39.5 %custom-call.76 = f32[4,128,128]{1,2,0:T(8,128)S(1)} custom-call(f32[4,128,128]{2,1,0:T(8,128)S(1)} %get-tuple-element.127), custom_call_target="InvertDiagBlocksLowerTriangular" | custom-call | tf_op jit(solution)/shard_map/while/body/jit(_solve_triangular)/triangular_solve | solution.py:605
  715.4 11.7 %custom-call.77 = f32[1,128,128]{2,1,0:T(8,128)S(1)} custom-call(f32[1,128,128]{2,1,0:T(8,128)S(1)} %cholesky.780), custom_call_target="Cholesky" | custom-call | tf_op jit(solution)/shard_map/while/body/jit(cholesky)/cholesky | solution.py:608
  727.3 9.8 %custom-call.78 = f32[1,1,128,128]{2,3,1,0:T(8,128)S(1)} custom-call(f32[1,1,128,128]{3,2,1,0:T(8,128)S(1)} %get-tuple-element.277), custom_call_target="InvertDiagBlocksLowerTriangular" | custom-call | tf_op jit(solution)/shard_map/while/body/jit(cholesky)/cholesky | solution.py:608
  741.1 11.7 %custom-call.79 = f32[1,128,128]{2,1,0:T(8,128)S(1)} custom-call(f32[1,128,128]{2,1,0:T(8,128)S(1)} %cholesky.784), custom_call_target="Cholesky" | custom-call | tf_op jit(solution)/shard_map/while/body/jit(cholesky)/cholesky | solution.py:608
  752.9 9.8 %custom-call.80 = f32[1,1,128,128]{2,3,1,0:T(8,128)S(1)} custom-call(f32[1,1,128,128]{3,2,1,0:T(8,128)S(1)} %get-tuple-element.274), custom_call_target="InvertDiagBlocksLowerTriangular" | custom-call | tf_op jit(solution)/shard_map/while/body/jit(cholesky)/cholesky | solution.py:608
  765.1 11.7 %custom-call.81 = f32[1,128,128]{2,1,0:T(8,128)S(1)} custom-call(f32[1,128,128]{2,1,0:T(8,128)S(1)} %cholesky.789), custom_call_target="Cholesky" | custom-call | tf_op jit(solution)/shard_map/while/body/jit(cholesky)/cholesky | solution.py:608
  776.9 10.0 %custom-call.82 = f32[1,1,128,128]{2,3,1,0:T(8,128)S(1)} custom-call(f32[1,1,128,128]{3,2,1,0:T(8,128)S(1)} %get-tuple-element.271), custom_call_target="InvertDiagBlocksLowerTriangular" | custom-call | tf_op jit(solution)/shard_map/while/body/jit(cholesky)/cholesky | solution.py:608
  788.3 11.7 %custom-call.83 = f32[1,128,128]{2,1,0:T(8,128)S(1)} custom-call(f32[1,128,128]{2,1,0:T(8,128)S(1)} %fusion.65), custom_call_target="Cholesky" | custom-call | tf_op jit(solution)/shard_map/while/body/jit(cholesky)/cholesky | solution.py:608
  806.7 23.2 %while.25 = (s32[]{:T(128)}, f32[1024,1024]{1,0:T(8,128)}, s32[8,2]{0,1:T(2,128)S(1)}, f32[8,128,128]{2,1,0:T(8,128)S(1)}, s32[]{:T(128)}) while((s32[]{:T(128)}, f32[1024,1024]{1,0:T(8,128)}, s32[8,2]{0,1:T(2,128)S(1)}, f32[8,128,128]{2,1,0:T(8,128)S(1)}, s32[]{:T(128)}) %tuple.181), condition=%wide.while_cond.1.clone, body=%wide.while_body.1.clone.sunk | while | flops 2 | bytes 131181 | solution.py:617
  829.9 78.8 %custom-call.84 = f32[8,128,128]{1,2,0:T(8,128)S(1)} custom-call(f32[8,128,128]{2,1,0:T(8,128)S(1)} %get-tuple-element.128), custom_call_target="InvertDiagBlocksLowerTriangular" | custom-call | tf_op jit(solution)/shard_map/while/body/jit(_solve_triangular)/triangular_solve | solution.py:617
  927.0 5.4 convolution_subtract_fusion.4
  933.1 6.1 convolution_subtract_fusion.2
  939.9 7.3 convolution_subtract_fusion.6
  (304 shorter events, 216.1 us)
Async XLA Ops:
  0.6 1.2 copy-start.2
  1.9 0.9 copy-start.3
  2.8 0.9 copy-start.4
  3.7 1.0 copy-start.5
  79.2 1.3 copy-start
  80.5 1.1 copy-start.1
  141.9 4.1 copy-start.28
  155.5 1.9 copy-start.7
  295.8 3.9 copy-start.24
  302.8 0.7 copy-start.15
  303.0 0.7 copy-start.17
  303.7 0.7 copy-start.19
  310.8 1.0 copy-start.13
  336.6 0.7 copy-start.21
  539.2 9.5 copy-start.11
  547.4 1.3 copy-start.23
  548.7 3.6 copy-start.12
  558.4 2.0 copy-start.8
  699.5 3.8 copy-start.25
  706.4 0.7 copy-start.16
  706.6 0.7 copy-start.18
  707.3 0.7 copy-start.20
  714.4 1.0 copy-start.14
  740.4 0.7 copy-start.22
  910.5 3.0 copy-start.6
  939.9 8.0 copy-start.26
  939.9 8.0 copy-start.27
  947.9 1.4 copy-start.9
  953.7 4.1 copy-start.10
  957.8 2.6 copy-start.33
  957.8 3.3 copy-start.32
  957.8 3.9 copy-start.34
  957.8 4.6 copy-start.31
  957.8 5.2 copy-start.30
  957.8 5.9 copy-start.29

commit v4 on v3

v4 whole, which is shorter than its diff:
```python
import functools
import math

import jax
import jax.numpy as jnp
from jax import lax
from jax.experimental import pallas as pl
from jax.experimental.pallas import tpu as pltpu
from jax.sharding import PartitionSpec as P

BETA_ONE = 0.9
BETA_TWO = 0.95
FACTOR_BETA = 0.9
ADAM_EPS = 1e-08
INNER_RATE = 0.5
OUTER_RATE = 0.7
OUTER_MOMENT = 0.9
RESIDUAL_LIMIT = 0.06

N = 1024
H = 512
Q4 = 256
ROUGH = 3
VMEM_LIMIT = 58 * 1024 * 1024
FINISH_LIMIT = 60 * 1024 * 1024


def nn(a, b):
    return jnp.dot(a, b, preferred_element_type=jnp.float32)


def nt(a, b):
    return lax.dot_general(a, b, (((1,), (1,)), ((), ())), preferred_element_type=jnp.float32)


def split(x):
    hi = x.astype(jnp.bfloat16)
    return hi, (x - hi.astype(jnp.float32)).astype(jnp.bfloat16)


def nt3(a, b):
    return nt(a[0], b[0]) + (nt(a[0], b[1]) + nt(a[1], b[0]))


def nn3(a, b):
    return nn(a[0], b[0]) + (nn(a[0], b[1]) + nn(a[1], b[0]))


def iotas(n):
    return lax.broadcasted_iota(jnp.int32, (n, n), 0), lax.broadcasted_iota(jnp.int32, (n, n), 1)


def low(e):
    r, c = iotas(e.shape[0])
    return jnp.where(r > c, e, jnp.where(r == c, 0.5 * e, 0.0))


def minus_eye(e):
    r, c = iotas(e.shape[0])
    return jnp.where(r == c, e - 1.0, e)


def diag_rows(s):
    r, c = iotas(s.shape[0])
    picked = jnp.where(r == c, s, 0.0)
    return jnp.sum(picked, 1, keepdims=True), jnp.sum(picked, 0, keepdims=True)


def residual(x, s, y_ref):
    a, b = slice(0, Q4), slice(Q4, H)
    if len(x) == 1:
        xa, x2 = x[0][a, a], x[0][b, :]
        ya = nn(xa, s[0][a, a]).astype(jnp.bfloat16)
        y2 = nn(x2, s[0][...]).astype(jnp.bfloat16)
        return nt(ya, xa), nt(y2[:, a], xa), nt(y2, x2)
    xa = (x[0][a, a], x[1][a, a])
    x2 = (x[0][b, :], x[1][b, :])
    ya = split(nn3(xa, (s[0][a, a], s[1][a, a])))
    y2 = split(nn3(x2, (s[0][...], s[1][...])))
    y2a = (y2[0][:, a], y2[1][:, a])
    return nt3(ya, xa), nt3(y2a, xa), nt3(y2, x2)


def leaf(s_ref, x_ref, sh, sl, xh, xl):
    a, b = slice(0, Q4), slice(Q4, H)
    dc, dr = diag_rows(s_ref[...])
    dc, dr = lax.rsqrt(dc), lax.rsqrt(dr)
    sn = s_ref[...] * dc * dr
    hi, lo = split(sn)
    sh[...] = hi
    sl[...] = lo
    e0 = minus_eye(sn)
    f0 = low(e0)
    r, c = iotas(H)
    x0 = jnp.where(r == c, 1.0 - f0, -f0)
    x_ref[...] = x0
    xh[...] = x0.astype(jnp.bfloat16)

    def update(e, fine):
        eaa, eca, edd = e
        faa, fdd = low(eaa).astype(jnp.bfloat16), low(edd).astype(jnp.bfloat16)
        fca = eca.astype(jnp.bfloat16)
        xa, xc, xd = xh[a, a], xh[b, a], xh[b, b]
        na = x_ref[a, a] - nn(faa, xa)
        nc = x_ref[b, a] - (nn(fca, xa) + nn(fdd, xc))
        nd = x_ref[b, b] - nn(fdd, xd)
        x_ref[a, a] = na
        x_ref[b, a] = nc
        x_ref[b, b] = nd
        if not fine:
            xh[a, a] = na.astype(jnp.bfloat16)
            xh[b, a] = nc.astype(jnp.bfloat16)
            xh[b, b] = nd.astype(jnp.bfloat16)

    def step(_, carry):
        eaa, eca, edd = residual((xh,), (sh,), None)
        update((minus_eye(eaa), eca, minus_eye(edd)), False)
        return carry

    lax.fori_loop(0, ROUGH, step, 0)
    hi, lo = split(x_ref[...])
    xh[...] = hi
    xl[...] = lo
    eaa, eca, edd = residual((xh, xl), (sh, sl), None)
    eaa, edd = minus_eye(eaa), minus_eye(edd)
    left = jnp.sum(eaa * eaa) + 2.0 * jnp.sum(eca * eca) + jnp.sum(edd * edd)
    update((eaa, eca, edd), True)
    x_ref[...] = x_ref[...] * dr
    hi, lo = split(x_ref[...])
    xh[...] = hi
    xl[...] = lo
    return left


WIDE = 640


MESH_ID = pl.DeviceIdType.MESH


def place():
    f = lax.axis_index("fsdp")
    return f // 8, (f // 2) % 4, f % 2


def to_device(x, z, core):
    return {"fsdp": (x * 4 + z) * 2 + core}


def greet(peers):
    barrier = pltpu.get_barrier_semaphore()
    for peer in peers:
        pl.semaphore_signal(barrier, inc=1, device_id=peer, device_id_type=MESH_ID)
    pl.semaphore_wait(barrier, len(peers))


def remote(src, dst, sends, recvs, index, peer):
    return pltpu.make_async_remote_copy(
        src_ref=src,
        dst_ref=dst,
        send_sem=sends.at[index],
        recv_sem=recvs.at[index],
        device_id=peer,
        device_id_type=MESH_ID,
    )


def rows_at(start, count):
    return pl.ds(pl.multiple_of(start, count), count)


def start_all(copies):
    for copy in copies:
        copy.start()


def wait_recv_all(copies):
    for copy in copies:
        copy.wait_recv()


def step_body(
    scale, act_in, grads_in, lf_in, rf_in, mom_in, msq_in, lb_in, rb_in, par_in, anc_in, om_in,
    p_own, p_other, mine_out, got_out, first_all,
    msq_out, left_next, right_next, anchor_out, momentum_out, res_out,
    act, grads, lf, rf, mom, msq, lb, rb, par, anc, om,
    g, fac, act2, flip, part, sent_c, got_c, sent_x, got_x, acc_x, sent_z, got_z, sent_f, twice,
    turned, seen, out32, whole, gm, bo, ff, p_ref, pt, q_ref, kept, upd, isl, res_own, res_got,
    s_ref, a21, x_ref, sh, sl, xh, xl, l21h, l21l, sends, recvs, local,
):
    bf, f32 = jnp.bfloat16, jnp.float32
    pairs = (
        (act_in, act), (grads_in, grads), (lf_in, lf), (rf_in, rf), (mom_in, mom), (msq_in, msq),
        (lb_in, lb), (rb_in, rb), (par_in, par), (anc_in, anc), (om_in, om),
    )
    loads = [pltpu.make_async_copy(src, dst, local.at[i]) for i, (src, dst) in enumerate(pairs)]
    start_all(loads)

    def arrive(i):
        loads[i].wait()

    fsdp, island, tensor = lax.axis_index("fsdp"), lax.axis_index("island"), lax.axis_index("tensor")
    x, z, core = place()
    partner = to_device(x, z, 1 - core)
    peers_x = [to_device((x + d) % 4, z, core) for d in (1, 2, 3)]
    peers_z = [to_device(x, (z + d) % 4, core) for d in (1, 2, 3)]
    peers_y = [{"island": (island + d) % 4} for d in (1, 2, 3)]
    other = {"tensor": 1 - tensor}
    chip = (x * 4 + z) * 64
    f, h = slice(0, H), slice(H, N)
    a, b = slice(0, Q4), slice(Q4, H)
    greet([partner, other] + peers_x + peers_z + peers_y)
    started = []

    def launch(copies):
        start_all(copies)
        started.extend(copies)
        return copies

    def tile(i):
        return rows_at(i * Q4, Q4)

    arrive(0)
    swap = launch([remote(act, act2, sends, recvs, 0, other)])

    arrive(2)
    arrive(3)
    near = pl.ds(pl.multiple_of(chip // 128 * 128, 128), WIDE)

    def pack(factor):
        narrow = factor[...].astype(jnp.bfloat16)
        twice[:, :N] = narrow
        twice[:, N:] = narrow
        return twice[:, near]

    @pl.when(core == 0)
    def _():
        fac[rows_at(chip, 32), :] = pack(lf)
        sent_f[...] = pack(rf)

    @pl.when(core == 1)
    def _():
        fac[rows_at(chip + 32, 32), :] = pack(rf)
        sent_f[...] = pack(lf)

    fac_c = launch([remote(sent_f, fac.at[rows_at(chip + core * 32, 32)], sends, recvs, 1, partner)])

    def multiply(o, source):
        flip[...] = source[...].T
        sent_c[o] = nn(flip[rows_at((1 - core) * 256, 256), :], grads[...]).astype(jnp.bfloat16)
        copies = launch([remote(sent_c.at[o], got_c.at[o], sends, recvs, 2 + o, partner)])
        part[o] = nn(flip[rows_at(core * 256, 256), :], grads[...])
        return copies

    def reduce_x(o, copies):
        wait_recv_all(copies)
        part[o] += got_c[o].astype(jnp.float32)
        for d in (1, 2, 3):
            sent_x[o, d - 1] = part[o, rows_at((x + d) % 4 * 64, 64), :].astype(jnp.bfloat16)
        return launch([
            remote(sent_x.at[o, d], got_x.at[o, d], sends, recvs, 4 + o * 3 + d, peers_x[d]) for d in range(3)
        ])

    def reduce_z(o, copies):
        wait_recv_all(copies)
        total = part[o, rows_at(x * 64, 64), :]
        for d in range(3):
            total += got_x[o, d].astype(jnp.float32)
        acc_x[o] = total
        for d in (1, 2, 3):
            sent_z[o, d - 1] = acc_x[o, rows_at((z + d) % 4 * 16, 16), :].astype(jnp.bfloat16)
        return launch([
            remote(sent_z.at[o, d], got_z.at[o, d], sends, recvs, 10 + o * 3 + d, peers_z[d]) for d in range(3)
        ])

    def base(o):
        half = tensor if o == 0 else 1 - tensor
        return half * 512 + core * 256

    def gather_z(o, copies):
        wait_recv_all(copies)
        total = acc_x[o, rows_at(z * 16, 16), :]
        for d in range(3):
            total += got_z[o, d].astype(jnp.float32)
        mine = rows_at(base(o) + x * 64 + z * 16, 16)
        g[mine, :] = (total * scale).astype(jnp.bfloat16)
        return launch([remote(g.at[mine], g.at[mine], sends, recvs, 16 + o * 3 + d, peers_z[d]) for d in range(3)])

    def gather_x(o, copies):
        wait_recv_all(copies)
        mine = rows_at(base(o) + x * 64, 64)
        return launch([remote(g.at[mine], g.at[mine], sends, recvs, 22 + o * 3 + d, peers_x[d]) for d in range(3)])

    def gather_c(o, copies):
        wait_recv_all(copies)
        mine = rows_at(base(o), 256)
        return launch([remote(g.at[mine], g.at[mine], sends, recvs, 28 + o, partner)])

    arrive(1)
    c0 = multiply(0, act)
    x0 = reduce_x(0, c0)
    z0 = reduce_z(0, x0)
    wait_recv_all(fac_c)
    mine_z = rows_at(chip, 64)
    fac_z = launch([remote(fac.at[mine_z], fac.at[mine_z], sends, recvs, 30 + d, peers_z[d]) for d in range(3)])
    wait_recv_all(swap)
    c1 = multiply(1, act2)
    gz0 = gather_z(0, z0)
    x1 = reduce_x(1, c1)
    wait_recv_all(fac_z)
    mine_x = rows_at(x * 256, 256)
    fac_x = launch([remote(fac.at[mine_x], fac.at[mine_x], sends, recvs, 33 + d, peers_x[d]) for d in range(3)])
    gx0 = gather_x(0, gz0)
    z1 = reduce_z(1, x1)
    gz1 = gather_z(1, z1)
    gx1 = gather_x(1, gz1)
    gc0 = gather_c(0, gx0)
    gc1 = gather_c(1, gx1)
    wait_recv_all(gc0)
    wait_recv_all(gc1)

    arrive(6)
    arrive(7)
    turned[...] = lb[:, pl.ds(pl.multiple_of(fsdp // 4 * 128, 128), 128)].T
    half = nn(turned[rows_at(fsdp % 4 * 32, 32), :], g[...]).astype(bf)
    rotated = nn(half, rb[...])
    arrive(4)
    arrive(5)
    first = BETA_ONE * mom[...] + (1.0 - BETA_ONE) * rotated
    second = BETA_TWO * msq[...] + (1.0 - BETA_TWO) * rotated * rotated
    msq_out[...] = second
    normed = (first / (jnp.sqrt(second) + ADAM_EPS)).astype(bf)
    first = first.astype(bf)

    @pl.when(core == 0)
    def _():
        seen[rows_at(chip, 32), :] = normed
        out32[...] = first
        gm[...] = g[...]
        bo[...] = lb[...]

    @pl.when(core == 1)
    def _():
        seen[rows_at(chip + 32, 32), :] = first
        out32[...] = normed
        gm[...] = g[...].T
        bo[...] = rb[...]

    seen_c = launch([remote(out32, seen.at[rows_at(chip + core * 32, 32)], sends, recvs, 40, partner)])

    def square_rows(i, c):
        ff[tile(i), :] = nt(gm[tile(i), :], gm[...]) * ((1.0 - FACTOR_BETA) / N)
        return c

    lax.fori_loop(0, 4, square_rows, 0)
    wait_recv_all(seen_c)
    mine = rows_at(chip, 64)
    seen_z = launch([remote(seen.at[mine], seen.at[mine], sends, recvs, 41 + d, peers_z[d]) for d in range(3)])
    away = rows_at(chip + (1 - core) * 32, 32)
    kept_c = launch([remote(ff.at[away], kept, sends, recvs, 45, partner)])

    wait_recv_all(fac_x)
    for i in range(8):
        for k in range(5):
            j = (i + k) % 8
            block = fac[i * 128:(i + 1) * 128, k * 128:(k + 1) * 128]
            whole[i * 128:(i + 1) * 128, j * 128:(j + 1) * 128] = block
            if 0 < k < 4:
                whole[j * 128:(j + 1) * 128, i * 128:(i + 1) * 128] = block.T

    def power_rows(i, c):
        nxt = (FACTOR_BETA * whole[tile(i), :].astype(f32) + ff[tile(i), :]).astype(bf)
        p_ref[tile(i), :] = nn(nxt, bo[...]).astype(bf)
        return c

    lax.fori_loop(0, 4, power_rows, 0)
    p_copy = pltpu.make_async_copy(p_ref, p_own, local.at[11])
    p_copy.start()
    p_swap = launch([remote(p_ref, p_other, sends, recvs, 44, partner)])

    pt[...] = p_ref[...].T
    s_ref[...] = nt(pt[f, :], pt[f, :])
    a21[...] = nt(pt[h, :], pt[f, :])
    r1 = leaf(s_ref, x_ref, sh, sl, xh, xl)

    wait_recv_all(seen_z)
    mine = rows_at(x * 256, 256)
    seen_x = launch([remote(seen.at[mine], seen.at[mine], sends, recvs, 46 + d, peers_x[d]) for d in range(3)])

    def by_x(t):
        ta = tuple(v[:, a] for v in t)
        xa, x2 = (xh[a, a], xl[a, a]), (xh[b, :], xl[b, :])
        if len(t) == 1:
            return nt(ta[0], xa[0]) + nt(ta[0], xa[1]), nt(t[0], x2[0]) + nt(t[0], x2[1])
        return nt3(ta, xa), nt3(t, x2)

    def l_rows(i, c):
        u, v = by_x(split(a21[tile(i), :]))
        l21h[tile(i), a], l21l[tile(i), a] = split(u)
        l21h[tile(i), b], l21l[tile(i), b] = split(v)
        return c

    lax.fori_loop(0, 2, l_rows, 0)
    s_ref[...] = nt(pt[h, :], pt[h, :]) - nt3((l21h[...], l21l[...]), (l21h[...], l21l[...]))

    def q1_rows(i, c):
        u, v = by_x((p_ref[tile(i), f],))
        q_ref[tile(i), a], pt[tile(i), a] = split(u)
        q_ref[tile(i), b], pt[tile(i), b] = split(v)
        return c

    lax.fori_loop(0, 4, q1_rows, 0)
    first_half, last_half = pl.ds(0, H), pl.ds(H, H)
    q1_copy = pltpu.make_async_copy(q_ref.at[:, first_half], mine_out.at[:, first_half], local.at[13])
    q1_copy.start()
    q1_swap = launch([remote(q_ref.at[:, first_half], got_out.at[:, first_half], sends, recvs, 49, partner)])

    wait_recv_all(kept_c)
    ours, theirs = ff[rows_at(chip + core * 32, 32), :], kept[...]
    left_next[...] = FACTOR_BETA * lf[...] + jnp.where(core == 0, ours, theirs)
    right_next[...] = FACTOR_BETA * rf[...] + jnp.where(core == 0, theirs, ours)

    r2 = leaf(s_ref, x_ref, sh, sl, xh, xl)
    res_own[...] = jnp.full((8, 128), jnp.maximum(r1, r2), f32)
    res_c = launch([remote(res_own, res_got, sends, recvs, 50, partner)])

    wait_recv_all(seen_x)
    upd_c = remote(upd.at[pl.ds(32, 32)], upd.at[pl.ds(32, 32)], sends, recvs, 51, partner)
    first_copy = pltpu.make_async_copy(seen, first_all, local.at[12])
    first_c = remote(seen, first_all, sends, recvs, 52, partner)

    @pl.when(core == 0)
    def _():
        back = nn(lb[rows_at(chip, 64), :], seen[...]).astype(bf)
        upd[...] = nt(back, rb[...])
        upd_c.start()

    @pl.when(core == 1)
    def _():
        first_copy.start()
        first_c.start()

    def q2_rows(i, c):
        t = p_ref[tile(i), h].astype(f32) - nt3((q_ref[tile(i), f], pt[tile(i), f]), (l21h[...], l21l[...]))
        u, v = by_x(split(t))
        q_ref[tile(i), H:H + Q4] = u.astype(bf)
        q_ref[tile(i), H + Q4:N] = v.astype(bf)
        return c

    lax.fori_loop(0, 4, q2_rows, 0)
    q2_copy = pltpu.make_async_copy(q_ref.at[:, last_half], mine_out.at[:, last_half], local.at[14])
    q2_copy.start()
    q2_swap = launch([remote(q_ref.at[:, last_half], got_out.at[:, last_half], sends, recvs, 53, partner)])

    @pl.when(core == 1)
    def _():
        upd_c.wait_recv()

    arrive(8)
    arrive(9)
    delta = anc[...] - (par[...] - INNER_RATE * upd[rows_at(core * 32, 32), :])
    isl[island] = delta
    isl_y = launch([remote(isl.at[island], isl.at[island], sends, recvs, 54 + d, peers_y[d]) for d in range(3)])


    wait_recv_all(isl_y)
    average = (isl[0] + isl[1] + isl[2] + isl[3]) / 4.0
    arrive(10)
    momentum = OUTER_MOMENT * om[...] + average
    momentum_out[...] = momentum
    anchor_out[...] = anc[...] - OUTER_RATE * (average + OUTER_MOMENT * momentum)
    wait_recv_all(res_c)
    res_out[...] = jnp.maximum(res_own[...], res_got[...])
    wait_recv_all(p_swap)
    wait_recv_all(q1_swap)
    wait_recv_all(q2_swap)
    p_copy.wait()
    q1_copy.wait()
    q2_copy.wait()

    @pl.when(core == 0)
    def _():
        first_c.wait_recv()
        upd_c.wait_send()

    @pl.when(core == 1)
    def _():
        first_copy.wait()
        first_c.wait_send()

    for copy in started:
        copy.wait_send()


def step(scale, operands):
    bf, f32 = jnp.bfloat16, jnp.float32
    vm, hbm = pl.BlockSpec(memory_space=pltpu.VMEM), pl.BlockSpec(memory_space=pl.ANY)
    square = jax.ShapeDtypeStruct((N, N), bf)
    strip = jax.ShapeDtypeStruct((32, N), f32)
    big = pltpu.VMEM((N, N), bf)
    thin = pltpu.VMEM((32, N), f32)
    return pl.pallas_call(
        functools.partial(step_body, scale),
        out_shape=(square,) * 5 + (strip,) * 5 + (jax.ShapeDtypeStruct((8, 128), f32),),
        in_specs=[hbm] * 11,
        out_specs=(hbm,) * 5 + (vm,) * 6,
        scratch_shapes=[
            pltpu.VMEM((512, 512), bf), pltpu.VMEM((512, N), bf), thin, thin, thin, thin, big, big, thin, thin, thin,
            big,
            pltpu.VMEM((N, WIDE), bf),
            pltpu.VMEM((512, 512), bf),
            pltpu.VMEM((512, 512), bf),
            pltpu.VMEM((2, 256, N), f32),
            pltpu.VMEM((2, 256, N), bf),
            pltpu.VMEM((2, 256, N), bf),
            pltpu.VMEM((2, 3, 64, N), bf),
            pltpu.VMEM((2, 3, 64, N), bf),
            pltpu.VMEM((2, 64, N), f32),
            pltpu.VMEM((2, 3, 16, N), bf),
            pltpu.VMEM((2, 3, 16, N), bf),
            pltpu.VMEM((32, WIDE), bf),
            pltpu.VMEM((32, 2 * N), bf),
            pltpu.VMEM((128, N), bf),
            big,
            pltpu.VMEM((32, N), bf),
            big, big, big,
            pltpu.VMEM((N, N), f32),
            big, big, big,
            thin,
            pltpu.VMEM((64, N), f32),
            pltpu.VMEM((4, 32, N), f32),
            pltpu.VMEM((8, 128), f32),
            pltpu.VMEM((8, 128), f32),
            pltpu.VMEM((H, H), f32), pltpu.VMEM((H, H), f32), pltpu.VMEM((H, H), f32),
        ] + [pltpu.VMEM((H, H), bf)] * 6 + [
            pltpu.SemaphoreType.DMA((57,)),
            pltpu.SemaphoreType.DMA((57,)),
            pltpu.SemaphoreType.DMA((15,)),
        ],
        compiler_params=pltpu.CompilerParams(
            collective_id=0, has_side_effects=True, vmem_limit_bytes=VMEM_LIMIT
        ),
        name="step",
    )(*operands)


def orth_columns(power, gram, work, flip, out):
    flip[...] = power[...].T

    def fill(i, c):
        rows = rows_at(i * 128, 128)
        gram[rows, :] = nt(flip[rows, :], flip[...])
        work[rows, :] = power[rows, :].astype(jnp.float32)
        return c

    lax.fori_loop(0, 8, fill, 0)
    lane = lax.broadcasted_iota(jnp.int32, (1, N), 1)

    def column(k, c):
        row = gram[pl.ds(k, 1), :]
        at = lane == k
        scale = 1.0 / jnp.sqrt(jnp.sum(jnp.where(at, row, 0.0), 1, keepdims=True))
        upper = jnp.where(lane >= k, row * scale, 0.0)
        after = jnp.where(at, 0.0, upper)

        def strip(i, c):
            rows = rows_at(i * 128, 128)
            old = gram[rows, :]
            gram[rows, :] = old - jnp.sum(jnp.where(at, old, 0.0), 1, keepdims=True) * scale * upper
            old = work[rows, :]
            done = jnp.sum(jnp.where(at, old, 0.0), 1, keepdims=True) * scale
            work[rows, :] = jnp.where(at, done, old - done * after)
            return c

        return lax.fori_loop(0, 8, strip, c)

    lax.fori_loop(0, N, column, 0)
    out[...] = work[...].astype(jnp.bfloat16)


def finish_body(
    p_own, p_other, mine, got, first_in, lb_in, rb_in, msq, left_next, right_next, anchor, momentum, res_in,
    anchor_out, momentum_out, moment_out, msq_out, lnext_out, rnext_out, left_out, right_out,
    lb, rb, first, left_v, right_v, rows, res, turned, mrows, gram, work, power, flip, local,
):
    fsdp = lax.axis_index("fsdp")
    core = fsdp % 2
    load_res, load_l, load_f, load_r = [
        pltpu.make_async_copy(src, dst, local.at[i])
        for i, (src, dst) in enumerate(((res_in, res), (lb_in, lb), (first_in, first), (rb_in, rb)))
    ]
    start_all([load_res, load_l])

    def twice(v, mm, m):
        both = mm(jnp.concatenate(split(v), 0), m[...])
        return both[:32] + both[32:]

    passed = [
        (
            pltpu.make_async_copy(src, rows.at[i], local.at[6 + i]),
            pltpu.make_async_copy(rows.at[i], dst, local.at[6 + i]),
        )
        for i, (src, dst) in enumerate((
            (anchor, anchor_out), (momentum, momentum_out), (msq, msq_out), (left_next, lnext_out), (right_next, rnext_out),
        ))
    ]
    for copy_in, _ in passed:
        copy_in.start()

    def close(left, right):
        outs = [
            pltpu.make_async_copy(left, left_out, local.at[11]),
            pltpu.make_async_copy(right, right_out, local.at[12]),
        ]
        start_all(outs)
        columns = pl.ds(pl.multiple_of(fsdp // 4 * 128, 128), 128)
        turned[...] = left[:, columns].T
        turn = nn(turned[rows_at(fsdp % 4 * 32, 32), :], lb[...])
        load_f.wait()
        part = twice(turn, nn, first)
        load_r.wait()
        part = twice(part, nt, rb)
        mrows[...] = twice(part, nn, right)
        last = pltpu.make_async_copy(mrows, moment_out, local.at[13])
        last.start()
        for copy_in, copy_out in passed:
            copy_in.wait()
            copy_out.start()
        for _, copy_out in passed:
            copy_out.wait()
        for copy in outs + [last]:
            copy.wait()

    def fetch(left, right):
        load_left = pltpu.make_async_copy(left, left_v, local.at[4])
        load_right = pltpu.make_async_copy(right, right_v, local.at[5])
        start_all([load_left, load_f, load_r, load_right])
        load_l.wait()
        load_left.wait()
        load_right.wait()

    load_res.wait()
    good = jnp.sum(res[...]) < RESIDUAL_LIMIT * 1024.0

    @pl.when(jnp.logical_and(good, core == 0))
    def _():
        fetch(mine, got)

    @pl.when(jnp.logical_and(good, core == 1))
    def _():
        fetch(got, mine)

    @pl.when(jnp.logical_not(good))
    def _():
        def redo(side, out):
            @pl.when(core == side)
            def _():
                pltpu.sync_copy(p_own, power)

            @pl.when(core != side)
            def _():
                pltpu.sync_copy(p_other, power)

            orth_columns(power, gram, work, flip, out)

        start_all([load_f, load_r])
        load_l.wait()
        redo(0, left_v)
        redo(1, right_v)

    close(left_v, right_v)


def finish(operands):
    bf, f32 = jnp.bfloat16, jnp.float32
    hbm = pl.BlockSpec(memory_space=pl.ANY)
    square = jax.ShapeDtypeStruct((N, N), bf)
    strip = jax.ShapeDtypeStruct((32, N), f32)
    big = pltpu.VMEM((N, N), bf)
    return pl.pallas_call(
        finish_body,
        out_shape=(strip,) * 6 + (square,) * 2,
        in_specs=[hbm] * 13,
        out_specs=(hbm,) * 8,
        scratch_shapes=[
            big, big, big, big, big, pltpu.VMEM((5, 32, N), f32), pltpu.VMEM((8, 128), f32),
            pltpu.VMEM((128, N), bf), pltpu.VMEM((32, N), f32),
            pltpu.VMEM((N, N), f32), pltpu.VMEM((N, N), f32), big, big,
            pltpu.SemaphoreType.DMA((14,)),
        ],
        compiler_params=pltpu.CompilerParams(vmem_limit_bytes=FINISH_LIMIT),
        name="finish",
    )(*operands)


def per_device(
    activations,
    out_grads,
    moment,
    moment_sq,
    left_factor,
    right_factor,
    left_basis,
    right_basis,
    params,
    anchor,
    outer_momentum,
):
    scale = 1.0 / math.sqrt(activations.shape[1] * lax.axis_size("fsdp"))
    left_old, right_old = left_basis[0, 0], right_basis[0, 0]
    operands = (
        activations[0], out_grads[0], left_factor[0, 0], right_factor[0, 0], moment[0, 0], moment_sq[0, 0],
        left_old, right_old, params[0, 0], anchor[0], outer_momentum[0],
    )
    power, power_other, mine, got, first_all, *rows, residual = step(scale, operands)
    anchor_next, momentum_next, moment_next, second_moment, left_next, right_next, left_new, right_new = finish(
        (power, power_other, mine, got, first_all, left_old, right_old, *rows, residual)
    )
    return (
        anchor_next[None],
        momentum_next[None],
        moment_next[None, None],
        second_moment[None, None],
        left_next[None, None],
        right_next[None, None],
        left_new[None, None],
        right_new[None, None],
    )


def solution(mesh):
    in_specs = (
        P("island", "fsdp", "tensor"),
        P("island", "fsdp", "tensor"),
        P("island", "tensor", "fsdp", None),
        P("island", "tensor", "fsdp", None),
        P("island", "tensor", "fsdp", None),
        P("island", "tensor", "fsdp", None),
        P("island", "tensor", None, None),
        P("island", "tensor", None, None),
        P("island", "tensor", "fsdp", None),
        P("tensor", "fsdp", None),
        P("tensor", "fsdp", None),
    )
    out_specs = (
        P("tensor", "fsdp", None),
        P("tensor", "fsdp", None),
        P("island", "tensor", "fsdp", None),
        P("island", "tensor", "fsdp", None),
        P("island", "tensor", "fsdp", None),
        P("island", "tensor", "fsdp", None),
        P("island", "tensor", None, None),
        P("island", "tensor", None, None),
    )
    return jax.shard_map(
        per_device, mesh=mesh, in_specs=in_specs, out_specs=out_specs, check_vma=False
    )
```

time: 971 us -> 3510 us (3.61)
  Pallas kernels: 135 us -> 3510 us
  other arithmetic: 571 us -> 0 us
  matrix products: 129 us -> 0 us
  local copies, waits for them, and re-layouts: 111 us -> 0 us
    pallas_call x2, Pallas kernels: 135 us -> 3510 us  [the longest x1 3380 us: finish(): pl.pallas_call(finish_body, out_shape=(strip,) * 6 + (square,) * 2, in_sp...]
    another operation x66 -> x0, other arithmetic: 559 us -> none  [the longest x5 163 us: exact_orth(): jax.scipy.linalg.solve_triangular(lower, power.T.astype(jnp.float32), low...]
    another operation x68 -> x0, matrix products: 108 us -> none  [the longest x30 76.5 us: exact_orth(): jax.scipy.linalg.solve_triangular(lower, power.T.astype(jnp.float32), low...]
    another operation x104 -> x0, local copies, waits for them, and re-layouts: 71.2 us -> none  [the longest x51 46.2 us: exact_orth(): jax.scipy.linalg.solve_triangular(lower, power.T.astype(jnp.float32), low...]
where the time goes in v4:
time: 3510 us
  Pallas kernels  3510 us (100%)
    pallas_call x1, Pallas kernels, finish(): pl.pallas_call(finish_body, out_shape=(strip,) * 6 + (square,) * 2, in_sp...  3380 us
    pallas_call x1, Pallas kernels, step(): pl.pallas_call(functools.partial(step_body, scale), out_shape=(square,) *...  130 us

profile of v4, /device:TPU:32, one launch (start us, length us, event | category | flops | bytes accessed | tf_op | source)
XLA Modules:
  0.0 3510.4 jit_solution(3291092266715863033)
XLA Ops:
  0.6 129.5 %step.1 = (bf16[1024,1024]{1,0:T(8,128)(2,1)}, bf16[1024,1024]{1,0:T(8,128)(2,1)}, bf16[1024,1024]{1,0:T(8,128)(2,1)}, bf16[1024,1024]{1,0:T(8,128)(2,1)}, bf16[...) custom-call(bf16[512,512]{1,0:T(8,128)(2,1)} %bitcast.24, ...), custom_call_target="tpu_custom_call" | custom-call | tf_op jit(solution)/shard_map/step/pallas_call | solution.py:502
  130.2 3380.1 %finish.1 = (f32[32,1024]{1,0:T(8,128)}, f32[32,1024]{1,0:T(8,128)}, f32[32,1024]{1,0:T(8,128)}, f32[32,1024]{1,0:T(8,128)}, f32[32,1024]{1,0:T(8,128)}, /*index...) custom-call(bf16[1024,1024]{1,0:T(8,128)(2,1)} %get-tuple-element.27.p_own, ...), custom_call_target="tpu_custom_call" | custom-call | tf_op jit(solution)/shard_map/finish/pallas_call | solution.py:680

commit v5 on v4

--- a/solution.py
+++ b/solution.py
@@ -300,20 +300,20 @@
     c0 = multiply(0, act)
     x0 = reduce_x(0, c0)
     z0 = reduce_z(0, x0)
+    wait_recv_all(swap)
+    c1 = multiply(1, act2)
     wait_recv_all(fac_c)
     mine_z = rows_at(chip, 64)
     fac_z = launch([remote(fac.at[mine_z], fac.at[mine_z], sends, recvs, 30 + d, peers_z[d]) for d in range(3)])
-    wait_recv_all(swap)
-    c1 = multiply(1, act2)
     gz0 = gather_z(0, z0)
     x1 = reduce_x(1, c1)
-    wait_recv_all(fac_z)
-    mine_x = rows_at(x * 256, 256)
-    fac_x = launch([remote(fac.at[mine_x], fac.at[mine_x], sends, recvs, 33 + d, peers_x[d]) for d in range(3)])
     gx0 = gather_x(0, gz0)
     z1 = reduce_z(1, x1)
     gz1 = gather_z(1, z1)
     gx1 = gather_x(1, gz1)
+    wait_recv_all(fac_z)
+    mine_x = rows_at(x * 256, 256)
+    fac_x = launch([remote(fac.at[mine_x], fac.at[mine_x], sends, recvs, 33 + d, peers_x[d]) for d in range(3)])
     gc0 = gather_c(0, gx0)
     gc1 = gather_c(1, gx1)
     wait_recv_all(gc0)

time: 3510 us -> 3510 us (level)
  no operation moved by 1% of the time
where the time goes in v5:
time: 3510 us
  Pallas kernels  3510 us (100%)
    pallas_call x1, Pallas kernels, finish(): pl.pallas_call(finish_body, out_shape=(strip,) * 6 + (square,) * 2, in_sp...  3380 us
    pallas_call x1, Pallas kernels, step(): pl.pallas_call(functools.partial(step_body, scale), out_shape=(square,) *...  126 us

profile of v5, /device:TPU:32, one launch (start us, length us, event | category | flops | bytes accessed | tf_op | source)
XLA Modules:
  0.0 3506.6 jit_solution(7399359813588620924)
XLA Ops:
  0.6 125.7 %step.1 = (bf16[1024,1024]{1,0:T(8,128)(2,1)}, bf16[1024,1024]{1,0:T(8,128)(2,1)}, bf16[1024,1024]{1,0:T(8,128)(2,1)}, bf16[1024,1024]{1,0:T(8,128)(2,1)}, bf16[...) custom-call(bf16[512,512]{1,0:T(8,128)(2,1)} %bitcast.24, ...), custom_call_target="tpu_custom_call" | custom-call | tf_op jit(solution)/shard_map/step/pallas_call | solution.py:502
  126.4 3380.1 %finish.1 = (f32[32,1024]{1,0:T(8,128)}, f32[32,1024]{1,0:T(8,128)}, f32[32,1024]{1,0:T(8,128)}, f32[32,1024]{1,0:T(8,128)}, f32[32,1024]{1,0:T(8,128)}, /*index...) custom-call(bf16[1024,1024]{1,0:T(8,128)(2,1)} %get-tuple-element.27.p_own, ...), custom_call_target="tpu_custom_call" | custom-call | tf_op jit(solution)/shard_map/finish/pallas_call | solution.py:680

commit v6 on v5

--- a/solution.py
+++ b/solution.py
@@ -314,14 +314,23 @@
     wait_recv_all(fac_z)
     mine_x = rows_at(x * 256, 256)
     fac_x = launch([remote(fac.at[mine_x], fac.at[mine_x], sends, recvs, 33 + d, peers_x[d]) for d in range(3)])
+    arrive(6)
+    arrive(7)
+    turned[...] = lb[:, pl.ds(pl.multiple_of(fsdp // 4 * 128, 128), 128)].T
+
+    @pl.when(core == 0)
+    def _():
+        bo[...] = lb[...]
+
+    @pl.when(core == 1)
+    def _():
+        bo[...] = rb[...]
+
     gc0 = gather_c(0, gx0)
     gc1 = gather_c(1, gx1)
     wait_recv_all(gc0)
     wait_recv_all(gc1)
 
-    arrive(6)
-    arrive(7)
-    turned[...] = lb[:, pl.ds(pl.multiple_of(fsdp // 4 * 128, 128), 128)].T
     half = nn(turned[rows_at(fsdp % 4 * 32, 32), :], g[...]).astype(bf)
     rotated = nn(half, rb[...])
     arrive(4)
@@ -337,14 +346,12 @@
         seen[rows_at(chip, 32), :] = normed
         out32[...] = first
         gm[...] = g[...]
-        bo[...] = lb[...]
 
     @pl.when(core == 1)
     def _():
         seen[rows_at(chip + 32, 32), :] = first
         out32[...] = normed
         gm[...] = g[...].T
-        bo[...] = rb[...]
 
     seen_c = launch([remote(out32, seen.at[rows_at(chip + core * 32, 32)], sends, recvs, 40, partner)])
 

time: 3510 us -> 3510 us (level)
  no operation moved by 1% of the time
where the time goes in v6:
time: 3510 us
  Pallas kernels  3510 us (100%)
    pallas_call x1, Pallas kernels, finish(): pl.pallas_call(finish_body, out_shape=(strip,) * 6 + (square,) * 2, in_sp...  3380 us
    pallas_call x1, Pallas kernels, step(): pl.pallas_call(functools.partial(step_body, scale), out_shape=(square,) *...  126 us

profile of v6, /device:TPU:32, one launch (start us, length us, event | category | flops | bytes accessed | tf_op | source)
XLA Modules:
  0.0 3506.4 jit_solution(1792638797513655078)
XLA Ops:
  0.6 125.5 %step.1 = (bf16[1024,1024]{1,0:T(8,128)(2,1)}, bf16[1024,1024]{1,0:T(8,128)(2,1)}, bf16[1024,1024]{1,0:T(8,128)(2,1)}, bf16[1024,1024]{1,0:T(8,128)(2,1)}, bf16[...) custom-call(bf16[512,512]{1,0:T(8,128)(2,1)} %bitcast.24, ...), custom_call_target="tpu_custom_call" | custom-call | tf_op jit(solution)/shard_map/step/pallas_call | solution.py:509
  126.2 3380.1 %finish.1 = (f32[32,1024]{1,0:T(8,128)}, f32[32,1024]{1,0:T(8,128)}, f32[32,1024]{1,0:T(8,128)}, f32[32,1024]{1,0:T(8,128)}, f32[32,1024]{1,0:T(8,128)}, /*index...) custom-call(bf16[1024,1024]{1,0:T(8,128)(2,1)} %get-tuple-element.27.p_own, ...), custom_call_target="tpu_custom_call" | custom-call | tf_op jit(solution)/shard_map/finish/pallas_call | solution.py:687
